TPU v7x, 256 devices: a whole 4x4x8 slice. The times are simulated.
256 devices in a mesh: dp: 8 (over z_lo, x), expert: 32 (over z_hi, y, core).
Axes of the slice: x: 4, y: 4, z: 8 (z_hi: 4, z_lo: 2; z = z_hi * 2 + z_lo), core: 2. Of those that a mesh axis runs over, the one named last changes fastest.
Arguments:
- tokens: bfloat16 [1024, 196, 768], P(('dp', 'expert')), may hold values from -40 to 40
- router: bfloat16 [768, 64], P(None, 'expert'), may hold values from -0.375 to 0.375
- w_in: bfloat16 [64, 768, 3072], P('expert', None, 'dp'), may hold values from -0.21875 to 0.21875
- w_out: bfloat16 [64, 3072, 768], P('expert', 'dp'), may hold values from -0.109375 to 0.109375
- cotangent: bfloat16 [1024, 196, 768], P(('dp', 'expert')), may hold values from -6 to 6
Outputs:
- mixed: bfloat16 [1024, 196, 768], P(('dp', 'expert'))
- tokens_grad: bfloat16 [1024, 196, 768], P(('dp', 'expert'))
- w_in_grad: float32 [64, 768, 3072], P('expert', None, 'dp')
- w_out_grad: float32 [64, 3072, 768], P('expert', 'dp')
- router_grad: float32 [768, 64], P(None, 'expert')
All inputs are finite; a program needn't handle non-finite values.
Results may differ from a plain program's by a relative error of at most 0.025.
Values may be sent and summed in bfloat16 or wider, within the bound.
A program may use at most 128 MiB of HBM per device.

v0:
```python
import jax
import jax.numpy as jnp
from jax import lax
from jax.sharding import PartitionSpec as P


def deliver(values):
    parted = lax.all_to_all(values, "expert", split_axis=1, concat_axis=0, tiled=True)
    return lax.all_gather(parted, "dp", axis=0, tiled=True)


def collect(term, local_rows):
    summed = lax.psum_scatter(
        term(jnp.int32(0), local_rows * lax.axis_size("dp")), "dp", scatter_dimension=0, tiled=True
    )
    return lax.all_to_all(
        summed.astype(jnp.bfloat16), "expert", split_axis=0, concat_axis=1, tiled=True
    )


def body(tokens, router, w_in, w_out, cotangent):
    single = jnp.float32
    router_full = lax.all_gather(router, "expert", axis=1, tiled=True)
    logits = jnp.einsum("bmd,ds->bms", tokens, router_full, preferred_element_type=single)
    dispatch = jax.nn.softmax(logits, axis=1)
    combine = jax.nn.softmax(logits, axis=2)
    dispatch_low = dispatch.astype(jnp.bfloat16)
    combine_low = combine.astype(jnp.bfloat16)
    slot_in = jnp.einsum(
        "bms,bmd->bsd", dispatch_low, tokens, preferred_element_type=single
    ).astype(jnp.bfloat16)
    slot_rows = deliver(slot_in)
    local_rows = slot_rows.shape[0] // lax.axis_size("dp")
    pre = jnp.einsum("nsd,sdf->nsf", slot_rows, w_in, preferred_element_type=single)
    act = jax.nn.gelu(pre).astype(jnp.bfloat16)

    def forward_term(start, count):
        return jnp.einsum("nsf,sfd->nsd", act, w_out, preferred_element_type=single)

    slot_out = collect(forward_term, local_rows)
    mixed = jnp.einsum("bms,bsd->bmd", combine_low, slot_out, preferred_element_type=single).astype(
        jnp.bfloat16
    )
    slot_grad = jnp.einsum(
        "bms,bmd->bsd", combine_low, cotangent, preferred_element_type=single
    ).astype(jnp.bfloat16)
    combine_grad = jnp.einsum("bmd,bsd->bms", cotangent, slot_out, preferred_element_type=single)
    grad_rows = deliver(slot_grad)
    act_grad = jnp.einsum("nsd,sfd->nsf", grad_rows, w_out, preferred_element_type=single)
    _, back = jax.vjp(jax.nn.gelu, pre)
    pre_grad = back(act_grad)[0].astype(jnp.bfloat16)
    w_out_grad = jnp.einsum("nsf,nsd->sfd", act, grad_rows, preferred_element_type=single)
    w_in_grad = jnp.einsum("nsd,nsf->sdf", slot_rows, pre_grad, preferred_element_type=single)

    def backward_term(start, count):
        return jnp.einsum("nsf,sdf->nsd", pre_grad, w_in, preferred_element_type=single)

    input_slots = collect(backward_term, local_rows)
    input_part = jnp.einsum(
        "bms,bsd->bmd", dispatch_low, input_slots, preferred_element_type=single
    )
    dispatch_grad = jnp.einsum("bmd,bsd->bms", tokens, input_slots, preferred_element_type=single)
    logit_grad = dispatch * (
        dispatch_grad - jnp.sum(dispatch * dispatch_grad, axis=1, keepdims=True)
    )
    logit_grad = logit_grad + combine * (
        combine_grad - jnp.sum(combine * combine_grad, axis=2, keepdims=True)
    )
    logit_low = logit_grad.astype(jnp.bfloat16)
    tokens_grad = (
        input_part
        + jnp.einsum("bms,ds->bmd", logit_low, router_full, preferred_element_type=single)
    ).astype(jnp.bfloat16)
    router_part = jnp.einsum("bmd,bms->ds", tokens, logit_low, preferred_element_type=single)
    router_whole = lax.psum(router_part, ("dp", "expert"))
    owned = router.shape[1]
    router_grad = lax.dynamic_slice_in_dim(router_whole, lax.axis_index("expert") * owned, owned, 1)
    return (mixed, tokens_grad, w_in_grad, w_out_grad, router_grad)


def solution(mesh):
    placed = (
        P(("dp", "expert"), None, None),
        P(None, "expert"),
        P("expert", None, "dp"),
        P("expert", "dp", None),
        P(("dp", "expert"), None, None),
    )
    return jax.shard_map(
        body,
        mesh=mesh,
        in_specs=placed,
        out_specs=(
            P(("dp", "expert"), None, None),
            P(("dp", "expert"), None, None),
            P("expert", None, "dp"),
            P("expert", "dp", None),
            P(None, "expert"),
        ),
        check_vma=False,
    )
```

profile of v0, /device:TPU:1, one launch (start us, length us, event | category | flops | bytes accessed | tf_op | source)
XLA Modules:
  0.0 630.0 jit_solution(552806186208876505)
XLA Ops:
  7.2 49.5 %all-gather = bf16[32,2,768]{2,1,0:T(2,128)(2,1)S(1)} all-gather(bf16[1,2,768]{2,1,0:T(2,128)(2,1)} %bitcast.93), channel_id=1, replica_groups=mesh['dp'=8,'expert'=32] {'expert'}, dimensions={0}, use_global_device_ids=true | all-gather | bytes 101376 | tf_op jit(solution)/shard_map/all_gather | solution.py:23
  56.8 1.8 fusion.30
  59.3 1.9 convolution_convert_fusion.2
  61.5 18.8 %all_to_all.72 = bf16[4,64,768]{2,0,1:T(4,128)(2,1)S(1)} all-to-all(bf16[4,64,768]{2,0,1:T(4,128)(2,1)S(1)} %copy.26), channel_id=1, replica_groups=mesh['dp'=8,'expert'=32] {'expert'}, dimensions={1} | all-to-all | bytes 786432 | tf_op jit(solution)/shard_map/all_to_all | solution.py:8
  82.9 23.5 %all_to_all.73 = bf16[4,64,768]{2,0,1:T(4,128)(2,1)S(1)} all-to-all(bf16[4,64,768]{2,0,1:T(4,128)(2,1)S(1)} %copy.31), channel_id=1, replica_groups=mesh['dp'=8,'expert'=32] {'expert'}, dimensions={1} | all-to-all | bytes 786432 | tf_op jit(solution)/shard_map/all_to_all | solution.py:8
  107.5 21.1 %all-gather.4.cloned.1.call-done = bf16[1024,2,768]{2,0,1:T(8,128)(2,1)} async-done(((bf16[128,2,768]{2,0,1:T(8,128)(2,1)}), bf16[1024,2,768]{2,0,1:T(8,128)(2,1)}) %all-gather.4.cloned.1.call-update) | async-done | bytes 3145744 | tf_op jit(solution)/shard_map/all_gather | solution.py:9
  128.6 5.4 fusion.49
  134.0 42.0 %all-gather.6.cloned.1.call-done = bf16[1024,2,768]{2,0,1:T(8,128)(2,1)} async-done(((bf16[128,2,768]{2,0,1:T(8,128)(2,1)}), bf16[1024,2,768]{2,0,1:T(8,128)(2,1)}) %all-gather.6.cloned.1.call-update) | async-done | bytes 3145744 | tf_op jit(solution)/shard_map/all_gather | solution.py:9
  175.9 6.4 %fusion.10 = bf16[1024,2,384]{2,0,1:T(8,128)(2,1)S(1)} fusion(f32[2,1024,384]{2,1,0:T(8,128)} %fusion.49, bf16[1024,2,768]{2,0,1:T(8,128)(2,1)} %all-gather.6.cloned.1.call-done, bf16[2,384,768]{2,1,0:T(8,128)(2,1)} %param.8), kind=kOutput, calls=%fused_computation.12 | convolution fusion | flops 1223688192 | bytes 9043968 | tf_op jit(solution)/shard_map/nsd,sfd->nsf/dot_general | solution.py:49
  182.4 1.2 copy-done.2
  183.6 4.5 convolution_bitcast_fusion
  188.1 1.2 copy-done.3
  189.3 6.4 %convolution_bitcast_fusion.1 = f32[1024,2,768]{2,0,1:T(8,128)} fusion(bf16[2,384,768]{2,1,0:T(8,128)(2,1)S(1)} %copy-done.3, f32[2,1024,384]{2,1,0:T(8,128)} %fusion.49), kind=kOutput, calls=%fused_computation.21 | convolution fusion | flops 1215037440 | bytes 10616832 | tf_op jit(solution)/shard_map/nsf,sfd->nsd/dot_general | solution.py:38
  195.8 70.3 %reduce-scatter.5.cloned.1.call-done = f32[128,2,768]{2,0,1:T(8,128)} async-done(((f32[1024,2,768]{2,0,1:T(8,128)}), f32[128,2,768]{2,0,1:T(8,128)}) %reduce-scatter.5.cloned.1.call-update) | async-done | bytes 786448 | tf_op jit(solution)/shard_map/reduce_scatter | solution.py:13
  266.1 1.2 convert_element_type.41
  267.2 1.2 copy.33
  268.4 9.4 %all-to-all-start.3 = ((bf16[128,2,768]{2,1,0:T(2,128)(2,1)}), bf16[128,2,768]{2,1,0:T(2,128)(2,1)S(1)}, u32[]{:S(2)}, u32[]{:S(2)}) async-start(bf16[128,2,768]{2,1,0:T(2,128)(2,1)} %copy.33), calls=%async_computation.5 | async-start | bytes 786432 | tf_op jit(solution)/shard_map/all_to_all | solution.py:16
  277.8 6.6 %fusion.44 = f32[2,384,768]{2,1,0:T(8,128)} fusion(bf16[1024,2,768]{2,0,1:T(8,128)(2,1)} %all-gather.6.cloned.1.call-done, f32[2,1024,384]{2,1,0:T(8,128)} %fusion.49), kind=kOutput, calls=%fused_computation.65 | convolution fusion | flops 1215037440 | bytes 8650752 | tf_op jit(solution)/shard_map/nsf,nsd->sfd/dot_general | solution.py:52
  284.4 64.5 %reduce-scatter.3.cloned.1.call-done = f32[128,2,768]{2,0,1:T(8,128)} async-done(((f32[1024,2,768]{2,0,1:T(8,128)}), f32[128,2,768]{2,0,1:T(8,128)}) %reduce-scatter.3.cloned.1.call-update) | async-done | bytes 786448 | tf_op jit(solution)/shard_map/reduce_scatter | solution.py:13
  348.9 1.2 convert_element_type.37
  351.2 9.2 %all-to-all-start.1 = ((bf16[128,2,768]{2,1,0:T(2,128)(2,1)}), bf16[128,2,768]{2,1,0:T(2,128)(2,1)S(1)}, u32[]{:S(2)}, u32[]{:S(2)}) async-start(bf16[128,2,768]{2,1,0:T(2,128)(2,1)} %copy.28), calls=%async_computation.2 | async-start | bytes 786432 | tf_op jit(solution)/shard_map/all_to_all | solution.py:16
  360.5 5.6 fusion.50
  366.5 2.5 convolution_bitcast_fusion.3
  369.0 2.3 fusion.37
  371.3 5.1 all-to-all-done.1
  377.7 3.2 convolution_bitcast_fusion.4
  380.9 2.9 add_convert_fusion
  383.8 1.6 convolution_convert_fusion
  385.4 2.8 copy.40
  388.2 1.5 copy.41
  389.6 232.5 %all-reduce.2.cloned.1.call-done = f32[768,64]{0,1:T(8,128)} async-done(((f32[768,64]{0,1:T(8,128)}), f32[768,64]{0,1:T(8,128)}) %all-reduce.2.cloned.1.call-update) | async-done | bytes 196624 | tf_op jit(solution)/shard_map/psum | solution.py:75
  622.1 1.3 constant_dynamic-slice_fusion
  (38 shorter events, 7.6 us)
Async XLA Ops:
  7.2 75.0 %copy-start = (bf16[4,196,768]{2,0,1:T(4,128)(2,1)S(1)}, bf16[4,196,768]{2,0,1:T(4,128)(2,1)}, u32[]{:S(2)}) copy-start(bf16[4,196,768]{2,0,1:T(4,128)(2,1)} %param.9) | copy-start | bytes 3612676
  7.2 121.4 %all-gather.4.cloned.1.call-start = ((), (), s32[]{:S(2)}) async-start(), calls=%async_computation.6 | async-start | bytes 3538944 | tf_op jit(solution)/shard_map/all_gather | solution.py:9
  81.3 94.6 %all-gather.6.cloned.1.call-start = ((), (), s32[]{:S(2)}) async-start(), calls=%async_computation.8 | async-start | bytes 3538944 | tf_op jit(solution)/shard_map/all_gather | solution.py:9
  82.2 46.4 %copy-start.1 = (bf16[2,768,384]{2,1,0:T(8,128)(2,1)S(1)}, bf16[2,768,384]{2,1,0:T(8,128)(2,1)}, u32[]{:S(2)}) copy-start(bf16[2,768,384]{2,1,0:T(8,128)(2,1)} %param.7) | copy-start | bytes 3538948
  107.4 158.7 %reduce-scatter.5.cloned.1.call-start = ((), (), s32[]{:S(2)}) async-start(), calls=%async_computation.9 | async-start | bytes 7077888 | tf_op jit(solution)/shard_map/reduce_scatter | solution.py:13
  182.4 1.2 copy-start.2
  188.1 1.3 copy-start.3
  188.1 160.8 %reduce-scatter.3.cloned.1.call-start = ((), (), s32[]{:S(2)}) async-start(), calls=%async_computation.7 | async-start | bytes 7077888 | tf_op jit(solution)/shard_map/reduce_scatter | solution.py:13
  268.4 82.8 %all-to-all-start.3 = ((bf16[128,2,768]{2,1,0:T(2,128)(2,1)}), bf16[128,2,768]{2,1,0:T(2,128)(2,1)S(1)}, u32[]{:S(2)}, u32[]{:S(2)}) async-start(bf16[128,2,768]{2,1,0:T(2,128)(2,1)} %copy.33), calls=%async_computation.5 | async-start | bytes 786432 | tf_op jit(solution)/shard_map/all_to_all | solution.py:16
  351.2 25.2 %all-to-all-start.1 = ((bf16[128,2,768]{2,1,0:T(2,128)(2,1)}), bf16[128,2,768]{2,1,0:T(2,128)(2,1)S(1)}, u32[]{:S(2)}, u32[]{:S(2)}) async-start(bf16[128,2,768]{2,1,0:T(2,128)(2,1)} %copy.28), calls=%async_computation.2 | async-start | bytes 786432 | tf_op jit(solution)/shard_map/all_to_all | solution.py:16
  360.4 261.7 %all-reduce.2.cloned.1.call-start = ((), (), s32[]{:S(2)}) async-start(), calls=%async_computation.10 | async-start | bytes 393216 | tf_op jit(solution)/shard_map/psum | solution.py:75
  369.0 8.4 %copy-start.5 = (f32[4,196,64]{1,2,0:T(8,128)S(1)}, f32[4,196,64]{1,2,0:T(8,128)}, u32[]{:S(2)}) copy-start(f32[4,196,64]{1,2,0:T(8,128)} %get-tuple-element.18) | copy-start | bytes 602116
  377.7 3.2 copy-start.4
Sparse Core Ops, SparseCore 0:
  81.5 47.0 all-gather.3
  131.0 44.9 all-gather.5
  188.2 77.8 reduce-scatter.4
  268.5 80.3 reduce-scatter.2
  381.0 241.0 all-reduce.1
where the time goes:
time: 631 us; the launch traced here: 630 us
  waiting for transfers between devices  436 us (69%)
  blocking collectives  91.9 us (15%)
  matrix products  51.9 us (8%)
  starting transfers between devices  18.8 us (3%)
  between operations  13.9 us (2%)
  local copies, waits for them, and re-layouts  13.8 us (2%)
    psum x1, waiting for transfers between devices, body(): router_whole = lax.psum(router_part, ('dp', 'expert'))  232 us
    reduce_scatter x2, waiting for transfers between devices, collect(): lax.psum_scatter(term(jnp.int32(0), local_rows * lax.axis_size('dp')), 'd...  135 us
    all_gather x2, waiting for transfers between devices, deliver(): return lax.all_gather(parted, 'dp', axis=0, tiled=True)  63.1 us
    all_gather x1, blocking collectives, body(): router_full = lax.all_gather(router, 'expert', axis=1, tiled=True)  49.5 us
    all_to_all x2, blocking collectives, deliver(): lax.all_to_all(values, 'expert', split_axis=1, concat_axis=0, tiled=True)  42.4 us
    all_to_all x2, starting transfers between devices, collect(): lax.all_to_all(summed.astype(jnp.bfloat16), 'expert', split_axis=0, conca...  18.6 us
  transfers between devices with their start and end apart: 7, of which 6 were waited for; matrix products, arithmetic and copies ran while one was open for 7% of the time, Pallas kernels for 0%

commit v1 on v0

v1 whole, which is shorter than its diff:
```python
import functools

import jax
import jax.numpy as jnp
from jax import lax
from jax.experimental import pallas as pl
from jax.experimental.pallas import tpu as pltpu
from jax.sharding import PartitionSpec as P

SINGLE = jnp.float32
LOW = jnp.bfloat16
MESH = pl.DeviceIdType.MESH
RING = 4


def remote(src, dst, send, recv, device):
    copy = pltpu.make_async_remote_copy(
        src_ref=src, dst_ref=dst, send_sem=send, recv_sem=recv, device_id=device, device_id_type=MESH
    )
    copy.start()
    return copy


def await_bytes(ref, sem):
    pltpu.make_async_copy(ref, ref, sem).wait()


def greet(devices):
    barrier = pltpu.get_barrier_semaphore()
    for device in devices:
        pl.semaphore_signal(barrier, inc=1, device_id=device, device_id_type=MESH)
    return barrier


def greet_experts(barrier, dp, ex, experts):
    def one(k, carry):
        pl.semaphore_signal(
            barrier, inc=1, device_id=(dp, lax.rem(ex + k, experts)), device_id_type=MESH
        )
        return carry

    lax.fori_loop(1, experts, one, 0)


def exchange(src, dst, send, recv, dp, ex, experts):
    def one(k, carry):
        to = lax.rem(ex + k, experts)
        pltpu.make_async_remote_copy(
            src_ref=src.at[to],
            dst_ref=dst.at[ex],
            send_sem=send,
            recv_sem=recv,
            device_id=(dp, to),
            device_id_type=MESH,
        ).start()
        return carry

    lax.fori_loop(1, experts, one, 0)


def gather_kernel(experts, own, whole, send, recv):
    dp, ex = lax.axis_index("dp"), lax.axis_index("expert")
    barrier = pltpu.get_barrier_semaphore()
    greet_experts(barrier, dp, ex, experts)
    pl.semaphore_wait(barrier, experts - 1)

    def one(k, carry):
        pltpu.make_async_remote_copy(
            src_ref=own,
            dst_ref=whole.at[ex],
            send_sem=send,
            recv_sem=recv,
            device_id=(dp, lax.rem(ex + k, experts)),
            device_id_type=MESH,
        ).start()
        return carry

    lax.fori_loop(1, experts, one, 0)
    whole[ex] = own[...]
    await_bytes(whole.at[pl.ds(0, experts - 1)], send)
    await_bytes(whole.at[pl.ds(0, experts - 1)], recv)


def gather_router(router, experts):
    d, owned = router.shape
    lanes = 128
    used = d * owned // lanes
    rows = -(-used // 16) * 16
    flat = jnp.pad(router.T.reshape(used, lanes), ((0, rows - used), (0, 0)))
    whole = pl.pallas_call(
        functools.partial(gather_kernel, experts),
        out_shape=jax.ShapeDtypeStruct((experts, rows, lanes), router.dtype),
        in_specs=[pl.BlockSpec(memory_space=pltpu.VMEM)],
        out_specs=pl.BlockSpec(memory_space=pltpu.VMEM),
        scratch_shapes=[pltpu.SemaphoreType.DMA, pltpu.SemaphoreType.DMA],
        compiler_params=pltpu.CompilerParams(collective_id=0, has_side_effects=True),
        name="gather_router",
    )(flat)
    return whole[:, :used].reshape(experts * owned, d)


def reduce_kernel(experts, shards, part, total, first, held, second, sems):
    dp, ex = lax.axis_index("dp"), lax.axis_index("expert")
    barrier = pltpu.get_barrier_semaphore()
    greet_experts(barrier, dp, ex, experts)

    def greet_dp(k, carry):
        pl.semaphore_signal(
            barrier, inc=1, device_id=(lax.rem(dp + k, shards), ex), device_id_type=MESH
        )
        return carry

    lax.fori_loop(1, shards, greet_dp, 0)
    pl.semaphore_wait(barrier, experts + shards - 2)
    exchange(part, first, sems.at[0], sems.at[1], dp, ex, experts)
    first[ex] = part[ex]
    await_bytes(first.at[pl.ds(0, experts - 1)], sems.at[0])
    await_bytes(first.at[pl.ds(0, experts - 1)], sems.at[1])
    held[...] = jnp.sum(first[...], axis=0)

    def one(k, carry):
        pltpu.make_async_remote_copy(
            src_ref=held,
            dst_ref=second.at[dp],
            send_sem=sems.at[2],
            recv_sem=sems.at[3],
            device_id=(lax.rem(dp + k, shards), ex),
            device_id_type=MESH,
        ).start()
        return carry

    lax.fori_loop(1, shards, one, 0)
    second[dp] = held[...]
    await_bytes(second.at[pl.ds(0, shards - 1)], sems.at[2])
    await_bytes(second.at[pl.ds(0, shards - 1)], sems.at[3])
    total[...] = jnp.sum(second[...], axis=0)


def reduce_router(part, experts, shards):
    slots, d = part.shape
    owned = slots // experts
    lanes = owned * d // 6
    blocks = jnp.pad(part.reshape(experts, 6, lanes), ((0, 0), (0, 2), (0, 0)))
    total = pl.pallas_call(
        functools.partial(reduce_kernel, experts, shards),
        out_shape=jax.ShapeDtypeStruct((8, lanes), SINGLE),
        in_specs=[pl.BlockSpec(memory_space=pltpu.VMEM)],
        out_specs=pl.BlockSpec(memory_space=pltpu.VMEM),
        scratch_shapes=[
            pltpu.VMEM((experts, 8, lanes), SINGLE),
            pltpu.VMEM((8, lanes), SINGLE),
            pltpu.VMEM((shards, 8, lanes), SINGLE),
            pltpu.SemaphoreType.DMA((4,)),
        ],
        compiler_params=pltpu.CompilerParams(collective_id=2, has_side_effects=True),
        name="reduce_router",
    )(blocks)
    return total[:6].reshape(owned, d).T


def gelu_and_slope(v):
    c = 0.7978845608028654
    square = v * v
    t = jnp.tanh(c * v * (1.0 + 0.044715 * square))
    half = 0.5 * (1.0 + t)
    slope = half + 0.5 * v * (1.0 - t * t) * (c * (1.0 + 3.0 * 0.044715 * square))
    return v * half, slope


def turn(lhs, rhs):
    return lax.dot_general(lhs, rhs, (((1,), (1,)), ((), ())), preferred_element_type=SINGLE)


def outer(lhs, rhs):
    return lax.dot_general(lhs, rhs, (((0,), (0,)), ((), ())), preferred_element_type=SINGLE)


def dot(lhs, rhs):
    return jnp.dot(lhs, rhs, preferred_element_type=SINGLE)


def expert_kernel(
    experts,
    images,
    msg_in,
    msg_grad,
    w_in,
    w_out,
    back_out,
    back_inp,
    w_in_grad,
    w_out_grad,
    got,
    rows,
    part,
    act,
    slope,
    pre_grad,
    far,
    near,
    over,
    ready,
    a2a_send,
    a2a_recv,
    ag_send,
    ag_recv,
    rs_send,
    far_recv,
    near_recv,
    over_recv,
):
    dp, ex = lax.axis_index("dp"), lax.axis_index("expert")
    x, z = lax.rem(dp, RING), dp // RING
    x_right, x_left = lax.rem(x + 1, RING), lax.rem(x + 3, RING)
    x_far = lax.rem(x + 2, RING)
    other = 1 - z
    partner = (other * RING + x, ex)
    right = (z * RING + x_right, ex)
    left = (z * RING + x_left, ex)
    own = dp
    mate = other * RING + x
    n_rows = experts * images
    half = rows.shape[-1] // 2

    barrier = greet((partner, right, left))
    greet_experts(barrier, dp, ex, experts)
    pl.semaphore_wait(barrier, experts + 2)

    for a, msg in ((0, msg_in), (1, msg_grad)):
        exchange(msg, got.at[a], a2a_send.at[a], a2a_recv.at[a], dp, ex, experts)
        got[a, ex] = msg[ex]

    def place(shape, row_axis):
        row = lax.broadcasted_iota(jnp.int32, shape, row_axis)
        col = lax.broadcasted_iota(jnp.int32, shape, 1 - row_axis)
        slot = (row >= n_rows).astype(jnp.int32)
        row = row - slot * n_rows
        image = lax.bitwise_and(row, images - 1)
        source = lax.shift_right_logical(row, images.bit_length() - 1)
        return col - (source * 4 * images + slot * images + image)

    def mark(distance, which):
        return (distance == which * 2 * images).astype(SINGLE).astype(LOW)

    def unpack(a):
        await_bytes(got.at[a, pl.ds(0, experts - 1)], a2a_recv.at[a])
        flat = got[a].reshape(experts * 4 * images, half)
        distance = place((2 * n_rows, experts * 4 * images), 0)
        for h in range(2):
            block = dot(mark(distance, h), flat).astype(LOW)
            for e in range(2):
                rows[a, e, own, :, h * half : (h + 1) * half] = block[e * n_rows : (e + 1) * n_rows]

    sent = []

    def send_block(a, e, p, to, slot):
        block = rows.at[a, e, p]
        sent.append(remote(block, block, ag_send.at[a, slot], ag_recv.at[a, e, p], to))

    def arrived(a, e, p):
        await_bytes(rows.at[a, e, p], ag_recv.at[a, e, p])

    def gather_own(a):
        for e in range(2):
            send_block(a, e, own, partner, 3 * e)
            send_block(a, e, own, right, 3 * e + 1)
            send_block(a, e, own, left, 3 * e + 2)

    def gather_mate(a):
        for e in range(2):
            arrived(a, e, mate)
            send_block(a, e, mate, right, 6 + 2 * e)
            send_block(a, e, mate, left, 7 + 2 * e)

    def gather_near(a):
        for k, ring in enumerate((z, other)):
            p = ring * RING + x_left
            arrived(a, 0, p)
            send_block(a, 0, p, right, 10 + 2 * k)
            p = ring * RING + x_right
            arrived(a, 1, p)
            send_block(a, 1, p, left, 11 + 2 * k)

    def near_rest(a):
        for ring in (z, other):
            arrived(a, 1, ring * RING + x_left)
            arrived(a, 0, ring * RING + x_right)

    def far_rest(a):
        for ring in (z, other):
            for e in range(2):
                arrived(a, e, ring * RING + x_far)

    def forward(e, p):
        pre = dot(rows[0, e, p], w_in[e])
        value, grade = gelu_and_slope(pre)
        value = value.astype(LOW)
        act[e, p] = value
        slope[e, p] = grade
        part[0, e, p] = dot(value, w_out[e]).astype(LOW)

    def backward(e, p):
        grad = turn(rows[1, e, p], w_out[e])
        grad = (grad * slope[e, p]).astype(LOW)
        pre_grad[e, p] = grad
        part[1, e, p] = turn(grad, w_in[e]).astype(LOW)

    def over_blocks(step, first, count):
        def one(k, carry):
            e, k = lax.rem(k, 2), k // 2
            ring, k = lax.rem(k, 2), k // 2
            step(e, ring * RING + lax.rem(x + first + 2 * k, RING))
            return carry

        lax.fori_loop(0, 4 * count, one, 0)

    def over_experts(step, p):
        def one(e, carry):
            step(e, p)
            return carry

        lax.fori_loop(0, 2, one, 0)

    def reduce_far(a):
        for ring in range(2):
            p = ring * RING + x_far
            for e, to in ((0, right), (1, left)):
                sent.append(
                    remote(
                        part.at[a, e, p],
                        far.at[a, e, ring],
                        rs_send.at[a, 2 * ring + e],
                        far_recv.at[a, e, ring],
                        to,
                    )
                )

    def send_near(a, e, ring, side):
        p = ring * RING + (x_right, x_left)[side]
        sent.append(
            remote(
                part.at[a, e, p],
                near.at[a, side, e, ring],
                rs_send.at[a, 4 + 4 * side + 2 * ring + e],
                near_recv.at[a, side, e, ring],
                (right, left)[side],
            )
        )

    def reduce_near(a):
        for ring in range(2):
            send_near(a, 1, ring, 0)
            send_near(a, 0, ring, 1)
        for ring in range(2):
            for e in range(2):
                p = ring * RING + (x_right, x_left)[e]
                await_bytes(far.at[a, e, ring], far_recv.at[a, e, ring])
                total = part[a, e, p].astype(SINGLE) + far[a, e, ring].astype(SINGLE)
                part[a, e, p] = total.astype(LOW)
                send_near(a, e, ring, e)

    def near_total(a, e, ring):
        for side in range(2):
            await_bytes(near.at[a, side, e, ring], near_recv.at[a, side, e, ring])
        return (
            part[a, e, ring * RING + x].astype(SINGLE)
            + near[a, 0, e, ring].astype(SINGLE)
            + near[a, 1, e, ring].astype(SINGLE)
        )

    def reduce_over(a):
        for e in range(2):
            part[a, e, mate] = near_total(a, e, other).astype(LOW)
            sent.append(
                remote(
                    part.at[a, e, mate],
                    over.at[a, e],
                    rs_send.at[a, 12 + e],
                    over_recv.at[a, e],
                    partner,
                )
            )

    def give_back(a, back):
        halves = ([], [])
        for e in range(2):
            total = near_total(a, e, z)
            await_bytes(over.at[a, e], over_recv.at[a, e])
            total = (total + over[a, e].astype(SINGLE)).astype(LOW)
            for h in range(2):
                halves[h].append(total[:, h * half : (h + 1) * half])
        distance = place((experts * 4 * images, 2 * n_rows), 1)
        block = sum(dot(mark(distance, h), jnp.concatenate(halves[h], axis=0)) for h in range(2))
        ready[a] = block.astype(LOW).reshape(experts, 4 * images, half)
        exchange(ready.at[a], back, a2a_send.at[2 + a], a2a_recv.at[2 + a], dp, ex, experts)
        back[ex] = ready[a, ex]

    unpack(0)
    gather_own(0)
    unpack(1)
    over_experts(forward, own)
    gather_mate(0)
    gather_own(1)
    over_experts(forward, mate)
    gather_near(0)
    gather_mate(1)
    near_rest(0)
    over_blocks(forward, 1, 2)
    far_rest(0)
    over_blocks(forward, 2, 1)
    reduce_far(0)
    gather_near(1)
    over_experts(backward, own)
    over_experts(backward, mate)
    reduce_near(0)
    near_rest(1)
    over_blocks(backward, 1, 2)
    far_rest(1)
    over_blocks(backward, 2, 1)
    reduce_far(1)
    reduce_over(0)
    reduce_near(1)
    give_back(0, back_out)

    def weights(e, carry):
        def flat(value):
            return value.reshape(value.shape[0] * value.shape[1], value.shape[2])

        w_out_grad[e] = outer(flat(act[e]), flat(rows[1, e]))
        w_in_grad[e] = outer(flat(rows[0, e]), flat(pre_grad[e]))
        return carry

    lax.fori_loop(0, 2, weights, 0)
    reduce_over(1)
    give_back(1, back_inp)
    for a, back in ((0, back_out), (1, back_inp)):
        await_bytes(back.at[pl.ds(0, experts - 1)], a2a_recv.at[2 + a])
    for k in range(4):
        await_bytes(got.at[0, pl.ds(0, experts - 1)], a2a_send.at[k])
    for copy in sent:
        copy.wait_send()


def run_experts(slot_in, slot_grad, w_in, w_out, experts):
    images, slots, d = slot_in.shape
    half = d // 2
    hidden = w_in.shape[2]
    n_rows = experts * images

    def messages(value):
        value = value.reshape(images, experts, 2, 2, half)
        return value.transpose(1, 3, 2, 0, 4).reshape(experts, 4 * images, half)

    def slots_of(value):
        value = value.reshape(experts, 2, 2, images, half)
        return value.transpose(3, 0, 2, 1, 4).reshape(images, slots, d)

    vmem = pl.BlockSpec(memory_space=pltpu.VMEM)
    message = jax.ShapeDtypeStruct((experts, 4 * images, half), LOW)
    dma = pltpu.SemaphoreType.DMA
    back_out, back_inp, w_in_grad, w_out_grad = pl.pallas_call(
        functools.partial(expert_kernel, experts, images),
        out_shape=[
            message,
            message,
            jax.ShapeDtypeStruct(w_in.shape, SINGLE),
            jax.ShapeDtypeStruct(w_out.shape, SINGLE),
        ],
        in_specs=[vmem] * 4,
        out_specs=[vmem] * 4,
        scratch_shapes=[
            pltpu.VMEM((2, experts, 4 * images, half), LOW),
            pltpu.VMEM((2, 2, 2 * RING, n_rows, d), LOW),
            pltpu.VMEM((2, 2, 2 * RING, n_rows, d), LOW),
            pltpu.VMEM((2, 2 * RING, n_rows, hidden), LOW),
            pltpu.VMEM((2, 2 * RING, n_rows, hidden), SINGLE),
            pltpu.VMEM((2, 2 * RING, n_rows, hidden), LOW),
            pltpu.VMEM((2, 2, 2, n_rows, d), LOW),
            pltpu.VMEM((2, 2, 2, 2, n_rows, d), LOW),
            pltpu.VMEM((2, 2, n_rows, d), LOW),
            pltpu.VMEM((2, experts, 4 * images, half), LOW),
            dma((4,)),
            dma((4,)),
            dma((2, 14)),
            dma((2, 2, 2 * RING)),
            dma((2, 14)),
            dma((2, 2, 2)),
            dma((2, 2, 2, 2)),
            dma((2, 2)),
        ],
        compiler_params=pltpu.CompilerParams(
            collective_id=1, has_side_effects=True, vmem_limit_bytes=56 * 1024 * 1024
        ),
        name="experts",
    )(messages(slot_in), messages(slot_grad), w_in, w_out)
    return slots_of(back_out), slots_of(back_inp), w_in_grad, w_out_grad


def body(experts, shards, tokens, router, w_in, w_out, cotangent):
    slots = gather_router(router, experts)
    logits = jnp.einsum("bmd,sd->bms", tokens, slots, preferred_element_type=SINGLE)
    dispatch = jax.nn.softmax(logits, axis=1)
    combine = jax.nn.softmax(logits, axis=2)
    dispatch_low = dispatch.astype(LOW)
    combine_low = combine.astype(LOW)
    slot_in = jnp.einsum(
        "bms,bmd->bsd", dispatch_low, tokens, preferred_element_type=SINGLE
    ).astype(LOW)
    slot_grad = jnp.einsum(
        "bms,bmd->bsd", combine_low, cotangent, preferred_element_type=SINGLE
    ).astype(LOW)
    slot_out, input_slots, w_in_grad, w_out_grad = run_experts(
        slot_in, slot_grad, w_in, w_out, experts
    )
    mixed = jnp.einsum("bms,bsd->bmd", combine_low, slot_out, preferred_element_type=SINGLE).astype(
        LOW
    )
    combine_grad = jnp.einsum("bmd,bsd->bms", cotangent, slot_out, preferred_element_type=SINGLE)
    input_part = jnp.einsum(
        "bms,bsd->bmd", dispatch_low, input_slots, preferred_element_type=SINGLE
    )
    dispatch_grad = jnp.einsum("bmd,bsd->bms", tokens, input_slots, preferred_element_type=SINGLE)
    logit_grad = dispatch * (
        dispatch_grad - jnp.sum(dispatch * dispatch_grad, axis=1, keepdims=True)
    )
    logit_grad = logit_grad + combine * (
        combine_grad - jnp.sum(combine * combine_grad, axis=2, keepdims=True)
    )
    logit_low = logit_grad.astype(LOW)
    router_part = jnp.einsum("bmd,bms->sd", tokens, logit_low, preferred_element_type=SINGLE)
    router_grad = reduce_router(router_part, experts, shards)
    tokens_grad = (
        input_part + jnp.einsum("bms,sd->bmd", logit_low, slots, preferred_element_type=SINGLE)
    ).astype(LOW)
    return (mixed, tokens_grad, w_in_grad, w_out_grad, router_grad)


def solution(mesh):
    placed = (
        P(("dp", "expert"), None, None),
        P(None, "expert"),
        P("expert", None, "dp"),
        P("expert", "dp", None),
        P(("dp", "expert"), None, None),
    )
    return jax.shard_map(
        functools.partial(body, mesh.shape["expert"], mesh.shape["dp"]),
        mesh=mesh,
        in_specs=placed,
        out_specs=(
            P(("dp", "expert"), None, None),
            P(("dp", "expert"), None, None),
            P("expert", None, "dp"),
            P("expert", "dp", None),
            P(None, "expert"),
        ),
        check_vma=False,
    )
```

time: 631 us -> 219 us (0.35)
  waiting for transfers between devices: 436 us -> 0 us
  Pallas kernels: 0 us -> 187 us
  blocking collectives: 91.9 us -> 0 us
  matrix products: 51.9 us -> 11.7 us
  starting transfers between devices: 18.8 us -> 0 us
  between operations: 13.9 us -> 0.85 us
    psum x1 -> x0, waiting for transfers between devices: 232 us -> none  [body(): router_whole = lax.psum(router_part, ('dp', 'expert'))]
    pallas_call x0 -> x3, Pallas kernels: none -> 187 us  [the longest x1 151 us: run_experts(): pl.pallas_call(functools.partial(expert_kernel, experts, images), out_sha...]
    reduce_scatter x2 -> x0, waiting for transfers between devices: 135 us -> none  [collect(): lax.psum_scatter(term(jnp.int32(0), local_rows * lax.axis_size('dp')), 'd...]
    all_gather x2 -> x0, waiting for transfers between devices: 63.1 us -> none  [deliver(): return lax.all_gather(parted, 'dp', axis=0, tiled=True)]
    all_gather x1 -> x0, blocking collectives: 49.5 us -> none  [body(): router_full = lax.all_gather(router, 'expert', axis=1, tiled=True)]
    all_to_all x2 -> x0, blocking collectives: 42.4 us -> none  [deliver(): lax.all_to_all(values, 'expert', split_axis=1, concat_axis=0, tiled=True)]
    dot_general x12 -> x6, matrix products: 47.6 us -> 7.17 us  [the longest x1 2.89 us: body(): jnp.einsum('bms,sd->bmd', logit_low, slots, preferred_element_type=SINGLE)]
    all_to_all x2 -> x0, starting transfers between devices: 18.6 us -> none  [collect(): lax.all_to_all(summed.astype(jnp.bfloat16), 'expert', split_axis=0, conca...]
  transfers between devices with their start and end apart: 7 -> 0, of which waited for: 6 -> 0; matrix products, arithmetic and copies ran while one was open for 7% -> 0% of each run, Pallas kernels for 0% -> 0%
where the time goes in v1:
time: 219 us
  Pallas kernels  187 us (85%)
  local copies, waits for them, and re-layouts  17.3 us (8%)
  matrix products  11.7 us (5%)
    pallas_call x1, Pallas kernels, run_experts(): pl.pallas_call(functools.partial(expert_kernel, experts, images), out_sha...  151 us
    pallas_call x1, Pallas kernels, reduce_router(): pl.pallas_call(functools.partial(reduce_kernel, experts, shards), out_sha...  19.4 us
    pallas_call x1, Pallas kernels, gather_router(): pl.pallas_call(functools.partial(gather_kernel, experts), out_shape=jax.S...  16.6 us
    unnamed x16, local copies, waits for them, and re-layouts  7.98 us

profile of v1, /device:TPU:1, one launch (start us, length us, event | category | flops | bytes accessed | tf_op | source)
XLA Modules:
  0.0 218.7 jit_solution(7055701959208932565)
XLA Ops:
  0.6 0.8 reshape.52
  1.4 0.6 pad.8.own
  2.0 16.6 %gather_router.1 = bf16[32,16,128]{2,1,0:T(8,128)(2,1)} custom-call(bf16[16,128]{1,0:T(8,128)(2,1)} %pad.8.own), custom_call_target="tpu_custom_call" | custom-call | tf_op jit(solution)/shard_map/gather_router/pallas_call | solution.py:90
  18.7 1.0 reshape.64
  19.7 0.5 convolution_bitcast_fusion.2
  20.2 0.7 fusion.32
  20.9 0.6 convolution_convert_fusion.2
  21.6 0.3 copy.49
  21.9 0.8 reshape.55.msg_in
  22.8 0.4 fusion.33
  23.1 1.7 convolution_convert_fusion.1
  24.9 0.3 copy.48
  25.2 0.8 reshape.57.msg_grad
  26.1 151.0 %experts.1 = (bf16[32,16,384]{2,1,0:T(8,128)(2,1)}, bf16[32,16,384]{2,1,0:T(8,128)(2,1)}, f32[2,768,384]{2,1,0:T(8,128)}, f32[2,384,768]{2,1,0:T(8,128)}) custom-call(bf16[32,16,384]{2,1,0:T(8,128)(2,1)} %reshape.55.msg_in, bf16[32,16,384]{2,1,0:T(8,128)(2,1)} %reshape.57.msg_grad, bf16[2,768,384]{2,1,0:T(8,128)(2,1)} %w_in.1, bf16[2,384,768]{2,1,0:T(8,128)(2,1)} %w_out.1), custom_call_target="tpu_custom_call" | custom-call | tf_op jit(solution)/shard_map/experts/pallas_call | solution.py:461
  177.1 1.1 reshape.58
  178.2 0.3 copy.27
  178.8 1.8 convolution_bitcast_fusion
  180.6 0.8 fusion.10
  182.3 0.5 convolution_bitcast_fusion.1
  183.0 1.0 convolution_bitcast_fusion.3
  184.0 0.7 pad.9.part
  184.7 19.4 %reduce_router.1 = f32[8,256]{1,0:T(8,128)} custom-call(f32[32,8,256]{2,1,0:T(8,128)} %pad.9.part), custom_call_target="tpu_custom_call" | custom-call | tf_op jit(solution)/shard_map/reduce_router/pallas_call | solution.py:144
  204.2 1.3 reshape.63
  205.5 2.3 %fusion.25 = f32[4,196,768]{2,1,0:T(8,128)} fusion(bf16[4,64,768]{2,1,0:T(8,128)(2,1)S(1)} %reshape.61, f32[4,64]{1,0:T(4,128)S(1)} %get-tuple-element.23, f32[4,196,64]{1,2,0:T(8,128)S(1)} %convolution_bitcast_fusion.2), kind=kOutput, calls=%fused_computation.37 | convolution fusion | flops 77221312 | bytes 3003392 | tf_op jit(solution)/shard_map/bms,bsd->bmd/dot_general | solution.py:519
  207.8 2.9 %add_convert_fusion = bf16[4,196,768]{2,1,0:T(8,128)(2,1)S(1)} fusion(f32[4,196,768]{2,1,0:T(8,128)} %fusion.25, bf16[64,768,1]{1,0,2:T(8,128)(2,1)S(1)} %reshape.64, f32[4,196,64]{1,2,0:T(8,128)} %fusion.10, f32[4,196,64]{1,2,0:T(8,128)} %copy-done.5, f32[4,196,64]{1,2,0:T(8,128)S(1)} %get-tuple-element.24, f32[4,64]{1,0:T(4,128)S(1)} %get-tuple-element.23), kind=kOutput, calls=%fused_computation.4 | convolution fusion | flops 78626240 | bytes 4314112 | tf_op jit(solution)/shard_map/bms,sd->bmd/dot_general | solution.py:533
  210.7 1.5 copy.33
  212.1 0.6 convolution_convert_fusion
  212.7 1.5 copy.32
  214.2 0.6 copy-done.2
  214.8 1.4 copy.52
  216.2 1.1 copy-done.1
  217.3 1.4 copy.53
  (17 shorter events, 1.6 us)
Async XLA Ops:
  0.6 19.1 %copy-start = (bf16[4,196,768]{2,0,1:T(4,128)(2,1)S(1)}, bf16[4,196,768]{2,0,1:T(4,128)(2,1)}, u32[]{:S(2)}) copy-start(bf16[4,196,768]{2,0,1:T(4,128)(2,1)} %param.5) | copy-start | bytes 3612676
  180.6 1.1 copy-start.3
  182.0 1.0 copy-start.4
  182.8 22.7 %copy-start.5 = (f32[4,196,64]{1,2,0:T(8,128)}, f32[4,196,64]{1,2,0:T(8,128)S(1)}, u32[]{:S(2)}) copy-start(f32[4,196,64]{1,2,0:T(8,128)S(1)} %convolution_bitcast_fusion.1) | copy-start | bytes 602116
  212.7 2.1 copy-start.2
  214.8 2.5 %copy-start.1 = (f32[2,384,768]{2,1,0:T(8,128)S(1)}, f32[2,384,768]{2,1,0:T(8,128)}, u32[]{:S(2)}) copy-start(f32[2,384,768]{2,1,0:T(8,128)} %get-tuple-element.35) | copy-start | bytes 7077892

commit v2 on v0

v2 whole, which is shorter than its diff:
```python
import functools

import jax
import jax.numpy as jnp
from jax import lax
from jax.experimental import pallas as pl
from jax.experimental.pallas import tpu as pltpu
from jax.sharding import PartitionSpec as P

SINGLE = jnp.float32
LOW = jnp.bfloat16
MESH = pl.DeviceIdType.MESH
RING = 4
Z_HIGH = 4
LANES = 128
CHUNK = 16


def remote(src, dst, send, recv, device):
    copy = pltpu.make_async_remote_copy(
        src_ref=src, dst_ref=dst, send_sem=send, recv_sem=recv, device_id=device, device_id_type=MESH
    )
    copy.start()
    return copy


def await_bytes(ref, sem):
    pltpu.make_async_copy(ref, ref, sem).wait()


def gelu_and_slope(v):
    c = 0.7978845608028654
    square = v * v
    t = jnp.tanh(c * v * (1.0 + 0.044715 * square))
    half = 0.5 * (1.0 + t)
    slope = half + 0.5 * v * (1.0 - t * t) * (c * (1.0 + 3.0 * 0.044715 * square))
    return v * half, slope


def turn(lhs, rhs):
    return lax.dot_general(lhs, rhs, (((1,), (1,)), ((), ())), preferred_element_type=SINGLE)


def outer(lhs, rhs):
    return lax.dot_general(lhs, rhs, (((0,), (0,)), ((), ())), preferred_element_type=SINGLE)


def dot(lhs, rhs):
    return jnp.dot(lhs, rhs, preferred_element_type=SINGLE)


def place_of(z_at, lane, x, experts):
    z_at = lax.rem(z_at + 4 * Z_HIGH, 2 * Z_HIGH)
    return (lax.rem(z_at, 2) * RING + x, (z_at // 2) * (experts // Z_HIGH) + lane)


def layer_kernel(
    experts,
    images,
    tokens_hbm,
    cotangent_hbm,
    router_own,
    w_in_hbm,
    w_out_hbm,
    mixed_hbm,
    tokens_grad_hbm,
    w_in_grad_hbm,
    w_out_grad_hbm,
    router_total,
    held,
    w_in,
    w_out,
    router_got,
    router,
    dispatch,
    combine,
    dispatch_low,
    combine_low,
    message,
    got,
    rows,
    part,
    act,
    slope,
    pre_grad,
    cross,
    far,
    near,
    over,
    ready,
    back,
    combine_term,
    w_in_grad,
    w_out_grad,
    result,
    router_message,
    router_first,
    router_mine,
    router_second,
    local,
    a2a_send,
    a2a_recv,
    ag_send,
    ag_recv,
    rs_send,
    cross_recv,
    far_recv,
    near_recv,
    over_recv,
):
    dp, ex = lax.axis_index("dp"), lax.axis_index("expert")
    shards = 2 * RING
    x, z = lax.rem(dp, RING), dp // RING
    x_right, x_left = lax.rem(x + 1, RING), lax.rem(x + 3, RING)
    x_far = lax.rem(x + 2, RING)
    other = 1 - z
    partner = (other * RING + x, ex)
    right = (z * RING + x_right, ex)
    left = (z * RING + x_left, ex)
    own = dp
    mate = other * RING + x
    n_rows = experts * images
    half = rows.shape[-1] // 2
    slots = 2 * experts
    pairs = images * slots
    n_tokens, n_padded = tokens_hbm.shape[0], held.shape[1]
    chunks = rows.shape[-1] // LANES
    inner = experts // Z_HIGH
    lane = lax.rem(ex, inner)
    z_at = (ex // inner) * 2 + z
    way = 1 - 2 * z

    loads = [
        pltpu.make_async_copy(src, dst, local.at[k])
        for k, (src, dst) in enumerate(
            (
                (tokens_hbm, held.at[0, pl.ds(0, n_tokens)]),
                (cotangent_hbm, held.at[1, pl.ds(0, n_tokens)]),
                (w_in_hbm, w_in),
                (w_out_hbm, w_out),
            )
        )
    ]
    for load in loads:
        load.start()

    barrier = pltpu.get_barrier_semaphore()

    def greet_experts(k, carry):
        step = k // inner
        step = step - (step // Z_HIGH) * (Z_HIGH + 2)
        to = place_of(z_at - step * way, lax.rem(lane + k, inner), x, experts)
        pl.semaphore_signal(barrier, inc=1, device_id=to, device_id_type=MESH)
        return carry

    def greet_shards(k, carry):
        to = (lax.rem(dp + k, shards), ex)
        pl.semaphore_signal(barrier, inc=1, device_id=to, device_id_type=MESH)
        return carry

    greeted = (Z_HIGH + 1) * inner
    lax.fori_loop(1, greeted, greet_experts, 0)
    lax.fori_loop(1, shards, greet_shards, 0)
    pl.semaphore_wait(barrier, greeted - 1 + shards - 1)

    def deliver(src, dst, k):
        def one(i, carry):
            step = i // inner
            to = place_of(
                z_at + step * way * (1 - 2 * lax.rem(step, 2)), lax.rem(lane + i, inner), x, experts
            )
            pltpu.make_async_remote_copy(
                src_ref=src.at[to[1]],
                dst_ref=dst.at[step * inner + lane],
                send_sem=a2a_send.at[k],
                recv_sem=a2a_recv.at[k],
                device_id=to,
                device_id_type=MESH,
            ).start()
            return carry

        lax.fori_loop(1, experts, one, 0)
        dst[lane] = src[ex]

    def collect(src_of, dst, k):
        def one(i, carry):
            step = i // inner
            there = lax.rem(lane + i, inner)
            pltpu.make_async_remote_copy(
                src_ref=src_of(step * inner + there),
                dst_ref=dst.at[ex],
                send_sem=a2a_send.at[k],
                recv_sem=a2a_recv.at[k],
                device_id=place_of(z_at - step * way, there, x, experts),
                device_id_type=MESH,
            ).start()
            return carry

        lax.fori_loop(1, experts, one, 0)

    def received(ref, k):
        await_bytes(ref.at[pl.ds(0, experts - 1)], a2a_recv.at[k])

    def iota(shape, axis):
        return lax.broadcasted_iota(jnp.int32, shape, axis)

    def bits(n):
        return n.bit_length() - 1

    def by_expert(row):
        slot = (row >= n_rows).astype(jnp.int32)
        row = row - slot * n_rows
        image = lax.bitwise_and(row, images - 1)
        return lax.shift_right_logical(row, bits(images)) * 4 * images + slot * images + image

    def by_image(row):
        slot = lax.bitwise_and(row, slots - 1)
        image = lax.shift_right_logical(row, bits(slots))
        odd = lax.bitwise_and(slot, 1)
        return lax.shift_right_logical(slot, 1) * 4 * images + odd * images + image

    def by_slot(row):
        odd = lax.bitwise_and(row, 1)
        return lax.shift_right_logical(row, 1) * CHUNK + odd * chunks

    def distance(shape, axis, order):
        return iota(shape, axis) - order(iota(shape, 1 - axis))

    def mark(distances, at):
        return (distances == at).astype(SINGLE).astype(LOW)

    def pack(value, order):
        n = value.shape[0]
        away = distance((experts * 4 * images, n), 0, order)
        block = sum(
            dot(mark(away, h * 2 * images), value[:, h * half : (h + 1) * half]) for h in range(2)
        )
        return block.astype(LOW).reshape(experts, 4 * images, half)

    def unpack(value, order, n):
        flat = value.reshape(experts * 4 * images, half)
        away = distance((n, experts * 4 * images), 1, order)
        return [dot(mark(away, h * 2 * images), flat).astype(LOW) for h in range(2)]

    collect(lambda block: router_own, router_got, 4)
    router_got[ex] = router_own[...]
    for load in loads[:2]:
        load.wait()
    if n_padded > n_tokens:
        for k in range(2):
            held[k, n_tokens:] = jnp.zeros((n_padded - n_tokens, held.shape[2]), LOW)
    received(router_got, 4)
    flat = router_got[...].reshape(experts * CHUNK, LANES)
    away = distance((slots, experts * CHUNK), 1, by_slot)
    for c in range(chunks):
        router[:, c * LANES : (c + 1) * LANES] = dot(mark(away, c), flat).astype(LOW)

    column = iota((slots, n_padded), 1)
    image_of = jnp.where(column < n_tokens, lax.bitwise_and(column, images - 1), -1)

    def per_image(reduce, value, fill):
        spread = jnp.zeros_like(value)
        for i in range(images):
            mine = image_of == i
            total = reduce(jnp.where(mine, value, fill), axis=1, keepdims=True)
            spread = jnp.where(mine, total, spread)
        return spread

    def apart(value, low):
        for i in range(images):
            low[i * slots : (i + 1) * slots] = jnp.where(image_of == i, value, 0.0).astype(LOW)

    def together(value):
        total = jnp.zeros((slots, n_padded), SINGLE)
        for i in range(images):
            total = jnp.where(image_of == i, value[i * slots : (i + 1) * slots], total)
        return total

    logits = turn(router[...], held[0])
    weight = jnp.exp(logits - per_image(jnp.max, logits, -jnp.inf))
    weight = jnp.where(image_of >= 0, weight, 0.0)
    weight = weight / jnp.where(image_of >= 0, per_image(jnp.sum, weight, 0.0), 1.0)
    dispatch[...] = weight
    apart(weight, dispatch_low)
    message[0] = pack(dot(dispatch_low[...], held[0]).astype(LOW), by_image)
    deliver(message.at[0], got.at[0], 0)
    weight = jnp.exp(logits - jnp.max(logits, axis=0, keepdims=True))
    weight = weight / jnp.sum(weight, axis=0, keepdims=True)
    combine[...] = weight
    apart(weight, combine_low)
    message[1] = pack(dot(combine_low[...], held[1]).astype(LOW), by_image)

    def own_rows(a):
        received(got.at[a], a)
        for h, block in enumerate(unpack(got[a], by_expert, 2 * n_rows)):
            for e in range(2):
                rows[a, e, own, :, h * half : (h + 1) * half] = block[e * n_rows : (e + 1) * n_rows]

    sent = []

    def send_block(a, e, p, to, slot):
        block = rows.at[a, e, p]
        sent.append(remote(block, block, ag_send.at[a, slot], ag_recv.at[a, e, p], to))

    def arrived(a, e, p):
        await_bytes(rows.at[a, e, p], ag_recv.at[a, e, p])

    def gather_own(a):
        for e in range(2):
            send_block(a, e, own, partner, 3 * e)
            send_block(a, e, own, right, 3 * e + 1)
            send_block(a, e, own, left, 3 * e + 2)

    def gather_mate(a):
        for e in range(2):
            arrived(a, e, mate)
            send_block(a, e, mate, right, 6 + 2 * e)
            send_block(a, e, mate, left, 7 + 2 * e)

    def gather_far(a):
        for e, p, to in ((0, z * RING + x_left, right), (1, z * RING + x_right, left)):
            arrived(a, e, p)
            send_block(a, e, p, to, 10 + e)

    def gather_cross(a):
        for e in range(2):
            arrived(a, e, z * RING + x_far)
            send_block(a, e, z * RING + x_far, partner, 12 + e)

    def near_rest(a):
        arrived(a, 1, z * RING + x_left)
        arrived(a, 0, z * RING + x_right)

    def near_other(a):
        for e in range(2):
            arrived(a, e, other * RING + x_left)
            arrived(a, e, other * RING + x_right)

    def cross_rest(a):
        for e in range(2):
            arrived(a, e, other * RING + x_far)

    def forward(e, p):
        pre = dot(rows[0, e, p], w_in[e])
        value, grade = gelu_and_slope(pre)
        value = value.astype(LOW)
        act[e, p] = value
        slope[e, p] = grade
        part[0, e, p] = dot(value, w_out[e]).astype(LOW)

    def backward(e, p):
        grad = turn(rows[1, e, p], w_out[e])
        grad = (grad * slope[e, p]).astype(LOW)
        pre_grad[e, p] = grad
        part[1, e, p] = turn(grad, w_in[e]).astype(LOW)

    def over_near(step, ring):
        def one(k, carry):
            step(lax.rem(k, 2), ring * RING + lax.rem(x + 1 + 2 * (k // 2), RING))
            return carry

        lax.fori_loop(0, 4, one, 0)

    def over_experts(step, p):
        def one(e, carry):
            step(e, p)
            return carry

        lax.fori_loop(0, 2, one, 0)

    def send_part(a, e, p, buffer, slot, recv, to):
        sent.append(remote(part.at[a, e, p], buffer, rs_send.at[a, slot], recv, to))

    def add(a, e, p, buffer, recv):
        await_bytes(buffer, recv)
        total = part[a, e, p].astype(SINGLE) + buffer[...].astype(SINGLE)
        part[a, e, p] = total.astype(LOW)

    def reduce_cross(a):
        for e in range(2):
            p = other * RING + x_far
            send_part(a, e, p, cross.at[a, e], e, cross_recv.at[a, e], partner)

    def reduce_far(a):
        for e, to in ((0, right), (1, left)):
            p = z * RING + x_far
            add(a, e, p, cross.at[a, e], cross_recv.at[a, e])
            send_part(a, e, p, far.at[a, e], 2 + e, far_recv.at[a, e], to)

    def send_near(a, e, ring, which, side):
        send_part(
            a,
            e,
            ring * RING + (x_right, x_left)[side],
            near.at[a, side, e, which],
            4 + 4 * side + 2 * which + e,
            near_recv.at[a, side, e, which],
            (right, left)[side],
        )

    def reduce_near_free(a):
        for e in range(2):
            for side in range(2):
                send_near(a, e, other, 1, side)
        for e in range(2):
            send_near(a, e, z, 0, 1 - e)

    def reduce_near(a):
        for e in range(2):
            add(a, e, z * RING + (x_right, x_left)[e], far.at[a, e], far_recv.at[a, e])
            send_near(a, e, z, 0, e)

    def near_total(a, e, ring, which):
        for side in range(2):
            await_bytes(near.at[a, side, e, which], near_recv.at[a, side, e, which])
        return (
            part[a, e, ring * RING + x].astype(SINGLE)
            + near[a, 0, e, which].astype(SINGLE)
            + near[a, 1, e, which].astype(SINGLE)
        )

    def reduce_over(a):
        for e in range(2):
            part[a, e, mate] = near_total(a, e, other, 1).astype(LOW)
            send_part(a, e, mate, over.at[a, e], 12 + e, over_recv.at[a, e], partner)

    def give_back(a):
        halves = ([], [])
        for e in range(2):
            total = near_total(a, e, z, 0)
            await_bytes(over.at[a, e], over_recv.at[a, e])
            total = (total + over[a, e].astype(SINGLE)).astype(LOW)
            halves[0].append(total)
        ready[a] = pack(jnp.concatenate(halves[0], axis=0), by_expert)
        collect(lambda block: ready.at[a, block], back.at[a], 2 + a)
        back[a, ex] = ready[a, lane]

    def given(a):
        received(back.at[a], 2 + a)
        return jnp.concatenate(unpack(back[a], by_image, pairs), axis=1)

    stores = []

    def store(src, dst, k):
        copy = pltpu.make_async_copy(src, dst, local.at[k])
        copy.start()
        stores.append(copy)

    def weights(e):
        def flat(value):
            return value.reshape(value.shape[0] * value.shape[1], value.shape[2])

        w_out_grad[e] = outer(flat(act[e]), flat(rows[1, e]))
        w_in_grad[e] = outer(flat(rows[0, e]), flat(pre_grad[e]))
        store(w_out_grad.at[e], w_out_grad_hbm.at[e], 4 + e)
        store(w_in_grad.at[e], w_in_grad_hbm.at[e], 6 + e)

    own_rows(0)
    gather_own(0)
    deliver(message.at[1], got.at[1], 1)
    for load in loads[2:]:
        load.wait()
    over_experts(forward, own)
    gather_mate(0)
    gather_far(0)
    over_experts(forward, mate)
    own_rows(1)
    gather_own(1)
    near_rest(0)
    over_near(forward, z)
    gather_cross(0)
    over_experts(forward, z * RING + x_far)
    near_other(0)
    over_near(forward, other)
    gather_mate(1)
    gather_far(1)
    reduce_near_free(0)
    cross_rest(0)
    over_experts(forward, other * RING + x_far)
    reduce_cross(0)
    over_experts(backward, own)
    over_experts(backward, mate)
    near_rest(1)
    over_near(backward, z)
    gather_cross(1)
    reduce_far(0)
    over_experts(backward, z * RING + x_far)
    near_other(1)
    over_near(backward, other)
    reduce_near(0)
    reduce_near_free(1)
    reduce_over(0)
    cross_rest(1)
    over_experts(backward, other * RING + x_far)
    reduce_cross(1)
    give_back(0)
    weights(0)
    reduce_far(1)
    reduce_over(1)
    weights(1)
    reduce_near(1)

    slot_out = given(0)
    result[0] = outer(combine_low[...], slot_out)[:n_tokens].astype(LOW)
    store(result.at[0], mixed_hbm, 8)
    grad = together(turn(slot_out, held[1]))
    weight = combine[...]
    combine_term[...] = weight * (grad - jnp.sum(weight * grad, axis=0, keepdims=True))

    give_back(1)
    input_slots = given(1)
    grad = together(turn(input_slots, held[0]))
    weight = dispatch[...]
    grad = weight * (grad - per_image(jnp.sum, weight * grad, 0.0)) + combine_term[...]
    grad = jnp.where(image_of >= 0, grad, 0.0).astype(LOW)
    total = dot(grad, held[0]).astype(LOW)
    away = distance((experts * CHUNK, slots), 0, by_slot)
    block = sum(
        dot(mark(away, c), total[:, c * LANES : (c + 1) * LANES]) for c in range(chunks)
    )
    router_message[...] = block.astype(LOW).reshape(experts, CHUNK, LANES)
    deliver(router_message, router_first, 5)
    value = outer(dispatch_low[...], input_slots) + outer(grad, router[...])
    result[1] = value[:n_tokens].astype(LOW)
    store(result.at[1], tokens_grad_hbm, 9)

    received(router_first, 5)
    router_mine[...] = jnp.sum(router_first[...].astype(SINGLE), axis=0)

    def share(k, carry):
        pltpu.make_async_remote_copy(
            src_ref=router_mine,
            dst_ref=router_second.at[dp],
            send_sem=a2a_send.at[6],
            recv_sem=a2a_recv.at[6],
            device_id=(lax.rem(dp + k, shards), ex),
            device_id_type=MESH,
        ).start()
        return carry

    lax.fori_loop(1, shards, share, 0)
    router_second[dp] = router_mine[...]
    await_bytes(router_second.at[pl.ds(0, shards - 1)], a2a_recv.at[6])
    router_total[...] = jnp.sum(router_second[...], axis=0)

    for k in range(4):
        await_bytes(got.at[0, pl.ds(0, experts - 1)], a2a_send.at[k])
    for k in range(4, 6):
        await_bytes(router_got.at[pl.ds(0, experts - 1)], a2a_send.at[k])
    await_bytes(router_second.at[pl.ds(0, shards - 1)], a2a_send.at[6])
    for copy in sent:
        copy.wait_send()
    for copy in stores:
        copy.wait()


def body(experts, tokens, router, w_in, w_out, cotangent):
    images, n, d = tokens.shape
    hidden = w_in.shape[2]
    owned = router.shape[1]
    slots = experts * owned
    n_tokens = images * n
    n_padded = -(-n_tokens // LANES) * LANES
    n_rows = experts * images
    used = d * owned // LANES
    half = d // 2

    def flat(value):
        return value.transpose(1, 0, 2).reshape(n_tokens, d)

    def unflat(value):
        return value.reshape(n, images, d).transpose(1, 0, 2)

    def low(*shape):
        return pltpu.VMEM(shape, LOW)

    def single(*shape):
        return pltpu.VMEM(shape, SINGLE)

    router_own = jnp.pad(router.T.reshape(used, LANES), ((0, CHUNK - used), (0, 0)))
    anywhere = pl.BlockSpec(memory_space=pl.ANY)
    vmem = pl.BlockSpec(memory_space=pltpu.VMEM)
    dma = pltpu.SemaphoreType.DMA
    mixed, tokens_grad, w_in_grad, w_out_grad, router_total = pl.pallas_call(
        functools.partial(layer_kernel, experts, images),
        out_shape=[
            jax.ShapeDtypeStruct((n_tokens, d), LOW),
            jax.ShapeDtypeStruct((n_tokens, d), LOW),
            jax.ShapeDtypeStruct(w_in.shape, SINGLE),
            jax.ShapeDtypeStruct(w_out.shape, SINGLE),
            jax.ShapeDtypeStruct((CHUNK, LANES), SINGLE),
        ],
        in_specs=[anywhere, anywhere, vmem, anywhere, anywhere],
        out_specs=[anywhere] * 4 + [vmem],
        scratch_shapes=[
            low(2, n_padded, d),
            low(*w_in.shape),
            low(*w_out.shape),
            low(experts, CHUNK, LANES),
            low(slots, d),
            single(slots, n_padded),
            single(slots, n_padded),
            low(images * slots, n_padded),
            low(images * slots, n_padded),
            low(2, experts, 4 * images, half),
            low(2, experts, 4 * images, half),
            low(2, 2, 2 * RING, n_rows, d),
            low(2, 2, 2 * RING, n_rows, d),
            low(2, 2 * RING, n_rows, hidden),
            single(2, 2 * RING, n_rows, hidden),
            low(2, 2 * RING, n_rows, hidden),
            low(2, 2, n_rows, d),
            low(2, 2, n_rows, d),
            low(2, 2, 2, 2, n_rows, d),
            low(2, 2, n_rows, d),
            low(2, experts, 4 * images, half),
            low(2, experts, 4 * images, half),
            single(slots, n_padded),
            single(*w_in.shape),
            single(*w_out.shape),
            low(2, n_tokens, d),
            low(experts, CHUNK, LANES),
            low(experts, CHUNK, LANES),
            single(CHUNK, LANES),
            single(2 * RING, CHUNK, LANES),
            dma((10,)),
            dma((7,)),
            dma((7,)),
            dma((2, 14)),
            dma((2, 2, 2 * RING)),
            dma((2, 14)),
            dma((2, 2)),
            dma((2, 2)),
            dma((2, 2, 2, 2)),
            dma((2, 2)),
        ],
        compiler_params=pltpu.CompilerParams(
            collective_id=0, has_side_effects=True, vmem_limit_bytes=58 * 1024 * 1024
        ),
        name="layer",
    )(flat(tokens), flat(cotangent), router_own, w_in, w_out)
    router_grad = router_total[:used].reshape(owned, d).T
    return (unflat(mixed), unflat(tokens_grad), w_in_grad, w_out_grad, router_grad)


def solution(mesh):
    placed = (
        P(("dp", "expert"), None, None),
        P(None, "expert"),
        P("expert", None, "dp"),
        P("expert", "dp", None),
        P(("dp", "expert"), None, None),
    )
    return jax.shard_map(
        functools.partial(body, mesh.shape["expert"]),
        mesh=mesh,
        in_specs=placed,
        out_specs=(
            P(("dp", "expert"), None, None),
            P(("dp", "expert"), None, None),
            P("expert", None, "dp"),
            P("expert", "dp", None),
            P(None, "expert"),
        ),
        check_vma=False,
    )
```

time: 631 us -> 174 us (0.28)
  waiting for transfers between devices: 436 us -> 0 us
  Pallas kernels: 0 us -> 156 us
  blocking collectives: 91.9 us -> 0 us
  matrix products: 51.9 us -> 0 us
  starting transfers between devices: 18.8 us -> 0 us
  between operations: 13.9 us -> 0.66 us
    psum x1 -> x0, waiting for transfers between devices: 232 us -> none  [body(): router_whole = lax.psum(router_part, ('dp', 'expert'))]
    pallas_call x0 -> x1, Pallas kernels: none -> 156 us  [body(): pl.pallas_call(functools.partial(layer_kernel, experts, images), out_shap...]
    reduce_scatter x2 -> x0, waiting for transfers between devices: 135 us -> none  [collect(): lax.psum_scatter(term(jnp.int32(0), local_rows * lax.axis_size('dp')), 'd...]
    all_gather x2 -> x0, waiting for transfers between devices: 63.1 us -> none  [deliver(): return lax.all_gather(parted, 'dp', axis=0, tiled=True)]
    dot_general x15 -> x0, matrix products: 51.9 us -> none  [the longest x1 6.64 us: body(): jnp.einsum('nsf,nsd->sfd', act, grad_rows, preferred_element_type=single)]
    all_gather x1 -> x0, blocking collectives: 49.5 us -> none  [body(): router_full = lax.all_gather(router, 'expert', axis=1, tiled=True)]
    all_to_all x2 -> x0, blocking collectives: 42.4 us -> none  [deliver(): lax.all_to_all(values, 'expert', split_axis=1, concat_axis=0, tiled=True)]
    all_to_all x2 -> x0, starting transfers between devices: 18.6 us -> none  [collect(): lax.all_to_all(summed.astype(jnp.bfloat16), 'expert', split_axis=0, conca...]
  transfers between devices with their start and end apart: 7 -> 0, of which waited for: 6 -> 0; matrix products, arithmetic and copies ran while one was open for 7% -> 0% of each run, Pallas kernels for 0% -> 0%
where the time goes in v2:
time: 174 us
  Pallas kernels  156 us (90%)
  local copies, waits for them, and re-layouts  17.1 us (10%)
    pallas_call x1, Pallas kernels, body(): pl.pallas_call(functools.partial(layer_kernel, experts, images), out_shap...  156 us
    reshape x2, local copies, waits for them, and re-layouts, unflat(): return value.reshape(n, images, d).transpose(1, 0, 2)  6.79 us
    reshape x2, local copies, waits for them, and re-layouts, flat(): return value.transpose(1, 0, 2).reshape(n_tokens, d)  4.47 us
    unnamed x10, local copies, waits for them, and re-layouts  3.93 us

profile of v2, /device:TPU:1, one launch (start us, length us, event | category | flops | bytes accessed | tf_op | source)
XLA Modules:
  0.0 174.0 jit_solution(17010002843288309002)
XLA Ops:
  0.6 0.7 reshape.30
  1.3 0.6 pad.4.router_own
  1.9 0.0 copy-start.2
  1.9 3.3 %reshape.28.tokens_hbm = bf16[784,768]{1,0:T(8,128)(2,1)} reshape(bf16[196,4,768]{2,1,0:T(4,128)(2,1)} %bitcast.7) | data formatting | bytes 2408448 | tf_op jit(solution)/shard_map/reshape | solution.py:569
  5.3 0.0 copy-done.2
  5.3 1.2 reshape.29.cotangent_hbm
  6.4 156.2 %layer.1 = (bf16[784,768]{1,0:T(8,128)(2,1)}, bf16[784,768]{1,0:T(8,128)(2,1)}, f32[2,768,384]{2,1,0:T(8,128)}, f32[2,384,768]{2,1,0:T(8,128)}, f32[16,128]{1,0:T(8,128)}) custom-call(bf16[784,768]{1,0:T(8,128)(2,1)} %reshape.28.tokens_hbm, bf16[784,768]{1,0:T(8,128)(2,1)} %reshape.29.cotangent_hbm, bf16[16,128]{1,0:T(8,128)(2,1)} %pad.4.router_own, ...), custom_call_target="tpu_custom_call" | custom-call | tf_op jit(solution)/shard_map/layer/pallas_call | solution.py:584
  162.7 0.0 copy-start.3
  162.7 3.3 %reshape.31 = bf16[196,4,768]{2,1,0:T(4,128)(2,1)} reshape(bf16[784,768]{1,0:T(8,128)(2,1)} %get-tuple-element.10) | data formatting | bytes 2408448 | tf_op jit(solution)/shard_map/reshape | solution.py:572
  166.0 0.0 copy-done.3
  166.0 0.6 reshape.33
  166.6 0.0 copy-start.1
  166.6 3.5 %reshape.32 = bf16[196,4,768]{2,1,0:T(4,128)(2,1)} reshape(bf16[784,768]{1,0:T(8,128)(2,1)} %get-tuple-element.11) | data formatting | bytes 2408448 | tf_op jit(solution)/shard_map/reshape | solution.py:572
  170.1 0.0 copy-done.1
  170.1 0.0 copy-start
  170.1 1.4 copy.12
  171.5 1.1 copy-done
  172.6 1.4 copy.13
Async XLA Ops:
  1.9 3.3 %copy-start.2 = (bf16[4,196,768]{2,0,1:T(4,128)(2,1)S(1)}, bf16[4,196,768]{2,0,1:T(4,128)(2,1)}, u32[]{:S(2)}) copy-start(bf16[4,196,768]{2,0,1:T(4,128)(2,1)} %param.9) | copy-start | bytes 3612676
  162.7 3.3 %copy-start.3 = (f32[16,128]{1,0:T(8,128)S(1)}, f32[16,128]{1,0:T(8,128)}, u32[]{:S(2)}) copy-start(f32[16,128]{1,0:T(8,128)} %get-tuple-element.14) | copy-start | bytes 24580
  166.6 3.5 %copy-start.1 = (f32[2,768,384]{2,1,0:T(8,128)S(1)}, f32[2,768,384]{2,1,0:T(8,128)}, u32[]{:S(2)}) copy-start(f32[2,768,384]{2,1,0:T(8,128)} %get-tuple-element.22) | copy-start | bytes 7077892
  170.1 2.5 %copy-start = (f32[2,384,768]{2,1,0:T(8,128)S(1)}, f32[2,384,768]{2,1,0:T(8,128)}, u32[]{:S(2)}) copy-start(f32[2,384,768]{2,1,0:T(8,128)} %get-tuple-element.23) | copy-start | bytes 7077892

commit v3 on v2

--- a/solution.py
+++ b/solution.py
@@ -67,9 +67,16 @@
     w_in_grad_hbm,
     w_out_grad_hbm,
     router_total,
+    raw,
     held,
     w_in,
     w_out,
+    mate_in,
+    mate_out,
+    give_in,
+    give_out,
+    took_in,
+    took_out,
     router_got,
     router,
     dispatch,
@@ -92,7 +99,6 @@
     combine_term,
     w_in_grad,
     w_out_grad,
-    result,
     router_message,
     router_first,
     router_mine,
@@ -100,8 +106,11 @@
     local,
     a2a_send,
     a2a_recv,
+    swap_send,
+    swap_recv,
     ag_send,
     ag_recv,
+    ag_far,
     rs_send,
     cross_recv,
     far_recv,
@@ -123,7 +132,7 @@
     half = rows.shape[-1] // 2
     slots = 2 * experts
     pairs = images * slots
-    n_tokens, n_padded = tokens_hbm.shape[0], held.shape[1]
+    n_tokens, n_padded = tokens_hbm.shape[0] * images, held.shape[1]
     chunks = rows.shape[-1] // LANES
     inner = experts // Z_HIGH
     lane = lax.rem(ex, inner)
@@ -134,8 +143,8 @@
         pltpu.make_async_copy(src, dst, local.at[k])
         for k, (src, dst) in enumerate(
             (
-                (tokens_hbm, held.at[0, pl.ds(0, n_tokens)]),
-                (cotangent_hbm, held.at[1, pl.ds(0, n_tokens)]),
+                (tokens_hbm, raw.at[0]),
+                (cotangent_hbm, raw.at[1]),
                 (w_in_hbm, w_in),
                 (w_out_hbm, w_out),
             )
@@ -161,7 +170,19 @@
     greeted = (Z_HIGH + 1) * inner
     lax.fori_loop(1, greeted, greet_experts, 0)
     lax.fori_loop(1, shards, greet_shards, 0)
+    for k in range(2):
+        loads[k].wait()
+        held[k, :n_tokens] = raw[k].reshape(n_tokens, held.shape[2])
+        if n_padded > n_tokens:
+            held[k, n_tokens:] = jnp.zeros((n_padded - n_tokens, held.shape[2]), LOW)
     pl.semaphore_wait(barrier, greeted - 1 + shards - 1)
+
+    for load in loads[2:]:
+        load.wait()
+    swaps = [
+        remote(w_in.at[0], mate_in, swap_send.at[0], swap_recv.at[0], partner),
+        remote(w_out.at[0], mate_out, swap_send.at[1], swap_recv.at[1], partner),
+    ]
 
     def deliver(src, dst, k):
         def one(i, carry):
@@ -244,11 +265,6 @@
 
     collect(lambda block: router_own, router_got, 4)
     router_got[ex] = router_own[...]
-    for load in loads[:2]:
-        load.wait()
-    if n_padded > n_tokens:
-        for k in range(2):
-            held[k, n_tokens:] = jnp.zeros((n_padded - n_tokens, held.shape[2]), LOW)
     received(router_got, 4)
     flat = router_got[...].reshape(experts * CHUNK, LANES)
     away = distance((slots, experts * CHUNK), 1, by_slot)
@@ -297,6 +313,9 @@
                 rows[a, e, own, :, h * half : (h + 1) * half] = block[e * n_rows : (e + 1) * n_rows]
 
     sent = []
+    bands = (pl.ds(0, n_rows // 2), pl.ds(n_rows // 2, n_rows // 2))
+    x_near = (x_left, x_right)
+    onward = (right, left)
 
     def send_block(a, e, p, to, slot):
         block = rows.at[a, e, p]
@@ -306,132 +325,169 @@
         await_bytes(rows.at[a, e, p], ag_recv.at[a, e, p])
 
     def gather_own(a):
-        for e in range(2):
-            send_block(a, e, own, partner, 3 * e)
-            send_block(a, e, own, right, 3 * e + 1)
-            send_block(a, e, own, left, 3 * e + 2)
+        send_block(a, 0, own, right, 0)
+        send_block(a, 0, own, left, 1)
+        send_block(a, 1, own, partner, 2)
+        send_block(a, 1, own, right, 3)
+        send_block(a, 1, own, left, 4)
 
     def gather_mate(a):
-        for e in range(2):
-            arrived(a, e, mate)
-            send_block(a, e, mate, right, 6 + 2 * e)
-            send_block(a, e, mate, left, 7 + 2 * e)
-
-    def gather_far(a):
-        for e, p, to in ((0, z * RING + x_left, right), (1, z * RING + x_right, left)):
+        arrived(a, 1, mate)
+        send_block(a, 1, mate, right, 5)
+        send_block(a, 1, mate, left, 6)
+
+    def gather_far(a, path):
+        e, ring = min(path, 1), (z, z, other)[path]
+        for side in range(2):
+            p = ring * RING + x_near[side]
             arrived(a, e, p)
-            send_block(a, e, p, to, 10 + e)
+            block = rows.at[a, e, p, bands[side]]
+            sent.append(
+                remote(
+                    block,
+                    block,
+                    ag_send.at[a, 7 + 2 * path + side],
+                    ag_far.at[a, path, side],
+                    onward[side],
+                )
+            )
+
+    def far_rest(a, path):
+        e, ring = min(path, 1), (z, z, other)[path]
+        for side in range(2):
+            await_bytes(rows.at[a, e, ring * RING + x_far, bands[side]], ag_far.at[a, path, side])
 
     def gather_cross(a):
-        for e in range(2):
-            arrived(a, e, z * RING + x_far)
-            send_block(a, e, z * RING + x_far, partner, 12 + e)
-
-    def near_rest(a):
-        arrived(a, 1, z * RING + x_left)
-        arrived(a, 0, z * RING + x_right)
+        send_block(a, 1, z * RING + x_far, partner, 11)
 
     def near_other(a):
-        for e in range(2):
-            arrived(a, e, other * RING + x_left)
-            arrived(a, e, other * RING + x_right)
-
-    def cross_rest(a):
-        for e in range(2):
-            arrived(a, e, other * RING + x_far)
-
-    def forward(e, p):
-        pre = dot(rows[0, e, p], w_in[e])
-        value, grade = gelu_and_slope(pre)
+        for side in range(2):
+            arrived(a, 1, other * RING + x_near[side])
+
+    def forward(p):
+        value, grade = gelu_and_slope(dot(rows[0, 1, p], w_in[1]))
         value = value.astype(LOW)
-        act[e, p] = value
-        slope[e, p] = grade
-        part[0, e, p] = dot(value, w_out[e]).astype(LOW)
-
-    def backward(e, p):
-        grad = turn(rows[1, e, p], w_out[e])
-        grad = (grad * slope[e, p]).astype(LOW)
-        pre_grad[e, p] = grad
-        part[1, e, p] = turn(grad, w_in[e]).astype(LOW)
-
-    def over_near(step, ring):
+        act[1, p] = value
+        slope[1, p] = grade
+        part[0, 1, p] = dot(value, w_out[1]).astype(LOW)
+
+    def backward(p):
+        grad = turn(rows[1, 1, p], w_out[1])
+        grad = (grad * slope[1, p]).astype(LOW)
+        pre_grad[1, p] = grad
+        part[1, 1, p] = turn(grad, w_in[1]).astype(LOW)
+
+    def near_ring(step, ring):
         def one(k, carry):
-            step(lax.rem(k, 2), ring * RING + lax.rem(x + 1 + 2 * (k // 2), RING))
+            step(ring * RING + lax.rem(x + 1 + 2 * k, RING))
             return carry
 
-        lax.fori_loop(0, 4, one, 0)
-
-    def over_experts(step, p):
-        def one(e, carry):
-            step(e, p)
+        lax.fori_loop(0, 2, one, 0)
+
+    def whole_ring(step):
+        def one(k, carry):
+            step(k)
             return carry
 
-        lax.fori_loop(0, 2, one, 0)
-
-    def send_part(a, e, p, buffer, slot, recv, to):
-        sent.append(remote(part.at[a, e, p], buffer, rs_send.at[a, slot], recv, to))
-
-    def add(a, e, p, buffer, recv):
-        await_bytes(buffer, recv)
-        total = part[a, e, p].astype(SINGLE) + buffer[...].astype(SINGLE)
-        part[a, e, p] = total.astype(LOW)
+        lax.fori_loop(0, RING, one, 0)
+
+    hidden = ((w_in.at[0], w_out.at[0]), (mate_in, mate_out))
+
+    def forward_both(k):
+        p = z * RING + k
+        total = 0.0
+        for h, (first, second) in enumerate(hidden):
+            value, grade = gelu_and_slope(dot(rows[0, 0, p], first[...]))
+            value = value.astype(LOW)
+            act[0, h * RING + k] = value
+            slope[0, h * RING + k] = grade
+            total = total + dot(value, second[...])
+        part[0, 0, p] = total.astype(LOW)
+
+    def backward_both(k):
+        p = z * RING + k
+        total = 0.0
+        for h, (first, second) in enumerate(hidden):
+            grad = turn(rows[1, 0, p], second[...])
+            grad = (grad * slope[0, h * RING + k]).astype(LOW)
+            pre_grad[0, h * RING + k] = grad
+            total = total + turn(grad, first[...])
+        part[1, 0, p] = total.astype(LOW)
+
+    def send_part(src, dst, send, recv, to):
+        sent.append(remote(src, dst, send, recv, to))
 
     def reduce_cross(a):
-        for e in range(2):
-            p = other * RING + x_far
-            send_part(a, e, p, cross.at[a, e], e, cross_recv.at[a, e], partner)
-
-    def reduce_far(a):
-        for e, to in ((0, right), (1, left)):
-            p = z * RING + x_far
-            add(a, e, p, cross.at[a, e], cross_recv.at[a, e])
-            send_part(a, e, p, far.at[a, e], 2 + e, far_recv.at[a, e], to)
-
-    def send_near(a, e, ring, which, side):
         send_part(
-            a,
-            e,
-            ring * RING + (x_right, x_left)[side],
-            near.at[a, side, e, which],
-            4 + 4 * side + 2 * which + e,
-            near_recv.at[a, side, e, which],
-            (right, left)[side],
+            part.at[a, 1, other * RING + x_far], cross, rs_send.at[a, 0], cross_recv.at[0], partner
         )
 
-    def reduce_near_free(a):
-        for e in range(2):
-            for side in range(2):
-                send_near(a, e, other, 1, side)
-        for e in range(2):
-            send_near(a, e, z, 0, 1 - e)
-
-    def reduce_near(a):
-        for e in range(2):
-            add(a, e, z * RING + (x_right, x_left)[e], far.at[a, e], far_recv.at[a, e])
-            send_near(a, e, z, 0, e)
-
-    def near_total(a, e, ring, which):
+    def add_cross(a):
+        p = z * RING + x_far
+        await_bytes(cross, cross_recv.at[0])
+        total = part[a, 1, p].astype(SINGLE) + cross[...].astype(SINGLE)
+        part[a, 1, p] = total.astype(LOW)
+
+    def reduce_far(a, path):
+        e, ring = min(path, 1), (z, z, other)[path]
         for side in range(2):
-            await_bytes(near.at[a, side, e, which], near_recv.at[a, side, e, which])
+            send_part(
+                part.at[a, e, ring * RING + x_far, bands[side]],
+                far.at[a, path, side],
+                rs_send.at[a, 1 + 2 * path + side],
+                far_recv.at[a, path, side],
+                onward[side],
+            )
+
+    def send_near(a, path, side, band):
+        e, ring = min(path, 1), (z, z, other)[path]
+        send_part(
+            part.at[a, e, ring * RING + x_near[1 - side], bands[band]],
+            near.at[a, path, side, bands[band]],
+            rs_send.at[a, 7 + 4 * path + 2 * side + band],
+            near_recv.at[a, path, side, band],
+            onward[side],
+        )
+
+    def near_free(a, path):
+        for side in range(2):
+            send_near(a, path, side, 1 - side)
+
+    def near_same(a, path):
+        for side in range(2):
+            send_near(a, path, side, side)
+
+    def near_summed(a, path):
+        e, ring = min(path, 1), (z, z, other)[path]
+        for side in range(2):
+            p = ring * RING + x_near[1 - side]
+            await_bytes(far.at[a, path, side], far_recv.at[a, path, side])
+            total = part[a, e, p, bands[side]].astype(SINGLE) + far[a, path, side].astype(SINGLE)
+            part[a, e, p, bands[side]] = total.astype(LOW)
+            send_near(a, path, side, side)
+
+    def near_total(a, path):
+        e, ring = min(path, 1), (z, z, other)[path]
+        for side in range(2):
+            for band in range(2):
+                await_bytes(near.at[a, path, side, bands[band]], near_recv.at[a, path, side, band])
         return (
             part[a, e, ring * RING + x].astype(SINGLE)
-            + near[a, 0, e, which].astype(SINGLE)
-            + near[a, 1, e, which].astype(SINGLE)
+            + near[a, path, 0].astype(SINGLE)
+            + near[a, path, 1].astype(SINGLE)
         )
 
     def reduce_over(a):
-        for e in range(2):
-            part[a, e, mate] = near_total(a, e, other, 1).astype(LOW)
-            send_part(a, e, mate, over.at[a, e], 12 + e, over_recv.at[a, e], partner)
+        part[a, 1, mate] = near_total(a, 2).astype(LOW)
+        send_part(part.at[a, 1, mate], over.at[a], rs_send.at[a, 19], over_recv.at[a], partner)
 
     def give_back(a):
-        halves = ([], [])
-        for e in range(2):
-            total = near_total(a, e, z, 0)
-            await_bytes(over.at[a, e], over_recv.at[a, e])
-            total = (total + over[a, e].astype(SINGLE)).astype(LOW)
-            halves[0].append(total)
-        ready[a] = pack(jnp.concatenate(halves[0], axis=0), by_expert)
+        first = near_total(a, 0)
+        second = near_total(a, 1)
+        await_bytes(over.at[a], over_recv.at[a])
+        second = second + over[a].astype(SINGLE)
+        total = jnp.concatenate([first.astype(LOW), second.astype(LOW)], axis=0)
+        ready[a] = pack(total, by_expert)
         collect(lambda block: ready.at[a, block], back.at[a], 2 + a)
         back[a, ex] = ready[a, lane]
 
@@ -446,63 +502,101 @@
         copy.start()
         stores.append(copy)
 
-    def weights(e):
-        def flat(value):
-            return value.reshape(value.shape[0] * value.shape[1], value.shape[2])
-
-        w_out_grad[e] = outer(flat(act[e]), flat(rows[1, e]))
-        w_in_grad[e] = outer(flat(rows[0, e]), flat(pre_grad[e]))
-        store(w_out_grad.at[e], w_out_grad_hbm.at[e], 4 + e)
-        store(w_in_grad.at[e], w_in_grad_hbm.at[e], 6 + e)
-
+    def flat(value):
+        return value.reshape(value.shape[0] * value.shape[1], value.shape[2])
+
+    def weights():
+        w_out_grad[1] = outer(flat(act[1]), flat(rows[1, 1]))
+        w_in_grad[1] = outer(flat(rows[0, 1]), flat(pre_grad[1]))
+        store(w_out_grad.at[1], w_out_grad_hbm.at[1], 5)
+        store(w_in_grad.at[1], w_in_grad_hbm.at[1], 7)
+
+    def weights_both():
+        mine = pl.ds(z * RING, RING)
+        halves = (pl.ds(0, RING), pl.ds(RING, RING))
+        give_out[...] = outer(flat(act[0, halves[1]]), flat(rows[1, 0, mine])).astype(LOW)
+        sent.append(remote(give_out, took_out, swap_send.at[2], swap_recv.at[2], partner))
+        give_in[...] = outer(flat(rows[0, 0, mine]), flat(pre_grad[0, halves[1]])).astype(LOW)
+        sent.append(remote(give_in, took_in, swap_send.at[3], swap_recv.at[3], partner))
+        w_out_grad[0] = outer(flat(act[0, halves[0]]), flat(rows[1, 0, mine]))
+        w_in_grad[0] = outer(flat(rows[0, 0, mine]), flat(pre_grad[0, halves[0]]))
+
+    def weights_taken():
+        await_bytes(took_out, swap_recv.at[2])
+        w_out_grad[0] = w_out_grad[0] + took_out[...].astype(SINGLE)
+        store(w_out_grad.at[0], w_out_grad_hbm.at[0], 4)
+        await_bytes(took_in, swap_recv.at[3])
+        w_in_grad[0] = w_in_grad[0] + took_in[...].astype(SINGLE)
+        store(w_in_grad.at[0], w_in_grad_hbm.at[0], 6)
+
+    far_ring = z * RING + x_far
+    far_other = other * RING + x_far
     own_rows(0)
     gather_own(0)
     deliver(message.at[1], got.at[1], 1)
-    for load in loads[2:]:
-        load.wait()
-    over_experts(forward, own)
+    forward(own)
     gather_mate(0)
-    gather_far(0)
-    over_experts(forward, mate)
+    gather_far(0, 1)
+    gather_far(0, 0)
+    forward(mate)
     own_rows(1)
     gather_own(1)
-    near_rest(0)
-    over_near(forward, z)
+    near_ring(forward, z)
+    far_rest(0, 1)
     gather_cross(0)
-    over_experts(forward, z * RING + x_far)
+    forward(far_ring)
     near_other(0)
-    over_near(forward, other)
+    near_ring(forward, other)
     gather_mate(1)
-    gather_far(1)
-    reduce_near_free(0)
-    cross_rest(0)
-    over_experts(forward, other * RING + x_far)
+    gather_far(1, 0)
+    gather_far(1, 1)
+    far_rest(0, 0)
+    await_bytes(mate_in, swap_recv.at[0])
+    await_bytes(mate_out, swap_recv.at[1])
+    whole_ring(forward_both)
+    reduce_far(0, 0)
+    near_free(0, 0)
+    near_free(0, 2)
+    near_same(0, 2)
+    near_free(0, 1)
+    gather_far(1, 2)
+    arrived(0, 1, far_other)
+    forward(far_other)
     reduce_cross(0)
-    over_experts(backward, own)
-    over_experts(backward, mate)
-    near_rest(1)
-    over_near(backward, z)
-    gather_cross(1)
-    reduce_far(0)
-    over_experts(backward, z * RING + x_far)
-    near_other(1)
-    over_near(backward, other)
-    reduce_near(0)
-    reduce_near_free(1)
+    backward(own)
+    backward(mate)
+    near_ring(backward, z)
+    far_rest(1, 0)
+    whole_ring(backward_both)
+    reduce_far(1, 0)
+    near_free(1, 0)
+    add_cross(0)
+    reduce_far(0, 1)
+    weights_both()
+    near_summed(0, 0)
+    far_rest(1, 1)
+    backward(far_ring)
+    reduce_far(1, 1)
+    near_free(1, 1)
+    near_ring(backward, other)
+    far_rest(1, 2)
+    backward(far_other)
+    reduce_far(1, 2)
+    near_free(1, 2)
+    near_summed(0, 1)
+    near_summed(1, 0)
     reduce_over(0)
-    cross_rest(1)
-    over_experts(backward, other * RING + x_far)
-    reduce_cross(1)
+    near_summed(1, 2)
+    near_summed(1, 1)
     give_back(0)
-    weights(0)
-    reduce_far(1)
     reduce_over(1)
-    weights(1)
-    reduce_near(1)
+    weights()
+    weights_taken()
 
     slot_out = given(0)
-    result[0] = outer(combine_low[...], slot_out)[:n_tokens].astype(LOW)
-    store(result.at[0], mixed_hbm, 8)
+    value = outer(combine_low[...], slot_out)[:n_tokens].astype(LOW)
+    raw[0] = value.reshape(raw.shape[1:])
+    store(raw.at[0], mixed_hbm, 8)
     grad = together(turn(slot_out, held[1]))
     weight = combine[...]
     combine_term[...] = weight * (grad - jnp.sum(weight * grad, axis=0, keepdims=True))
@@ -521,8 +615,8 @@
     router_message[...] = block.astype(LOW).reshape(experts, CHUNK, LANES)
     deliver(router_message, router_first, 5)
     value = outer(dispatch_low[...], input_slots) + outer(grad, router[...])
-    result[1] = value[:n_tokens].astype(LOW)
-    store(result.at[1], tokens_grad_hbm, 9)
+    raw[1] = value[:n_tokens].astype(LOW).reshape(raw.shape[1:])
+    store(raw.at[1], tokens_grad_hbm, 9)
 
     received(router_first, 5)
     router_mine[...] = jnp.sum(router_first[...].astype(SINGLE), axis=0)
@@ -548,7 +642,7 @@
     for k in range(4, 6):
         await_bytes(router_got.at[pl.ds(0, experts - 1)], a2a_send.at[k])
     await_bytes(router_second.at[pl.ds(0, shards - 1)], a2a_send.at[6])
-    for copy in sent:
+    for copy in swaps + sent:
         copy.wait_send()
     for copy in stores:
         copy.wait()
@@ -565,11 +659,8 @@
     used = d * owned // LANES
     half = d // 2
 
-    def flat(value):
-        return value.transpose(1, 0, 2).reshape(n_tokens, d)
-
-    def unflat(value):
-        return value.reshape(n, images, d).transpose(1, 0, 2)
+    def swap(value):
+        return value.transpose(1, 0, 2)
 
     def low(*shape):
         return pltpu.VMEM(shape, LOW)
@@ -584,8 +675,8 @@
     mixed, tokens_grad, w_in_grad, w_out_grad, router_total = pl.pallas_call(
         functools.partial(layer_kernel, experts, images),
         out_shape=[
-            jax.ShapeDtypeStruct((n_tokens, d), LOW),
-            jax.ShapeDtypeStruct((n_tokens, d), LOW),
+            jax.ShapeDtypeStruct((n, images, d), LOW),
+            jax.ShapeDtypeStruct((n, images, d), LOW),
             jax.ShapeDtypeStruct(w_in.shape, SINGLE),
             jax.ShapeDtypeStruct(w_out.shape, SINGLE),
             jax.ShapeDtypeStruct((CHUNK, LANES), SINGLE),
@@ -593,9 +684,16 @@
         in_specs=[anywhere, anywhere, vmem, anywhere, anywhere],
         out_specs=[anywhere] * 4 + [vmem],
         scratch_shapes=[
+            low(2, n, images, d),
             low(2, n_padded, d),
             low(*w_in.shape),
             low(*w_out.shape),
+            low(*w_in.shape[1:]),
+            low(*w_out.shape[1:]),
+            low(*w_in.shape[1:]),
+            low(*w_out.shape[1:]),
+            low(*w_in.shape[1:]),
+            low(*w_out.shape[1:]),
             low(experts, CHUNK, LANES),
             low(slots, d),
             single(slots, n_padded),
@@ -609,16 +707,15 @@
             low(2, 2 * RING, n_rows, hidden),
             single(2, 2 * RING, n_rows, hidden),
             low(2, 2 * RING, n_rows, hidden),
-            low(2, 2, n_rows, d),
-            low(2, 2, n_rows, d),
-            low(2, 2, 2, 2, n_rows, d),
-            low(2, 2, n_rows, d),
+            low(n_rows, d),
+            low(2, 3, 2, n_rows // 2, d),
+            low(2, 3, 2, n_rows, d),
+            low(2, n_rows, d),
             low(2, experts, 4 * images, half),
             low(2, experts, 4 * images, half),
             single(slots, n_padded),
             single(*w_in.shape),
             single(*w_out.shape),
-            low(2, n_tokens, d),
             low(experts, CHUNK, LANES),
             low(experts, CHUNK, LANES),
             single(CHUNK, LANES),
@@ -626,21 +723,24 @@
             dma((10,)),
             dma((7,)),
             dma((7,)),
-            dma((2, 14)),
+            dma((4,)),
+            dma((4,)),
+            dma((2, 13)),
             dma((2, 2, 2 * RING)),
-            dma((2, 14)),
-            dma((2, 2)),
-            dma((2, 2)),
-            dma((2, 2, 2, 2)),
-            dma((2, 2)),
+            dma((2, 3, 2)),
+            dma((2, 20)),
+            dma((1,)),
+            dma((2, 3, 2)),
+            dma((2, 3, 2, 2)),
+            dma((2,)),
         ],
         compiler_params=pltpu.CompilerParams(
             collective_id=0, has_side_effects=True, vmem_limit_bytes=58 * 1024 * 1024
         ),
         name="layer",
-    )(flat(tokens), flat(cotangent), router_own, w_in, w_out)
+    )(swap(tokens), swap(cotangent), router_own, w_in, w_out)
     router_grad = router_total[:used].reshape(owned, d).T
-    return (unflat(mixed), unflat(tokens_grad), w_in_grad, w_out_grad, router_grad)
+    return (swap(mixed), swap(tokens_grad), w_in_grad, w_out_grad, router_grad)
 
 
 def solution(mesh):

time: 174 us -> 171 us (0.983)
  local copies, waits for them, and re-layouts: 17.1 us -> 11.4 us
  Pallas kernels: 156 us -> 159 us
    reshape x4 -> x0, local copies, waits for them, and re-layouts: 11.3 us -> none  [the longest x2 6.79 us: unflat(): return value.reshape(n, images, d).transpose(1, 0, 2)]
    unnamed x10, local copies, waits for them, and re-layouts: 3.93 us -> 8.84 us
    pallas_call x1, Pallas kernels: 156 us -> 159 us  [body(): pl.pallas_call(functools.partial(layer_kernel, experts, images), out_shap...]
where the time goes in v3:
time: 171 us
  Pallas kernels  159 us (93%)
  local copies, waits for them, and re-layouts  11.4 us (7%)
    pallas_call x1, Pallas kernels, body(): pl.pallas_call(functools.partial(layer_kernel, experts, images), out_shap...  159 us
    unnamed x10, local copies, waits for them, and re-layouts  8.84 us

profile of v3, /device:TPU:1, one launch (start us, length us, event | category | flops | bytes accessed | tf_op | source)
XLA Modules:
  0.0 170.8 jit_solution(17534595583638306507)
XLA Ops:
  0.6 0.7 reshape.16
  1.3 0.6 pad.4.router_own
  1.9 158.7 %layer.1 = (bf16[196,4,768]{2,1,0:T(4,128)(2,1)}, bf16[196,4,768]{2,1,0:T(4,128)(2,1)}, f32[2,768,384]{2,1,0:T(8,128)}, f32[2,384,768]{2,1,0:T(8,128)}, f32[16,128]{1,0:T(8,128)}) custom-call(bf16[196,4,768]{2,1,0:T(4,128)(2,1)} %bitcast.9, bf16[196,4,768]{2,1,0:T(4,128)(2,1)} %bitcast.10, bf16[16,128]{1,0:T(8,128)(2,1)} %pad.4.router_own, ...), custom_call_target="tpu_custom_call" | custom-call | tf_op jit(solution)/shard_map/layer/pallas_call | solution.py:675
  160.7 1.3 reshape.17
  162.0 0.0 copy-start.2
  162.0 2.8 %copy.14 = bf16[4,196,768]{2,0,1:T(4,128)(2,1)} copy(bf16[4,196,768]{2,0,1:T(4,128)(2,1)} %bitcast.8) | data formatting | bytes 2408448
  164.8 0.0 copy-done.2
  164.8 0.0 copy-start.1
  164.8 1.0 copy.15
  165.8 1.1 copy-done.1
  166.9 0.0 copy-start
  166.9 1.4 copy.16
  168.3 1.1 copy-done
  169.4 1.4 copy.17
Async XLA Ops:
  162.0 2.8 %copy-start.2 = (bf16[196,4,768]{2,1,0:T(4,128)(2,1)S(1)}, bf16[196,4,768]{2,1,0:T(4,128)(2,1)}, u32[]{:S(2)}) copy-start(bf16[196,4,768]{2,1,0:T(4,128)(2,1)} %get-tuple-element.11) | copy-start | bytes 3612676
  164.8 2.1 %copy-start.1 = (f32[2,768,384]{2,1,0:T(8,128)S(1)}, f32[2,768,384]{2,1,0:T(8,128)}, u32[]{:S(2)}) copy-start(f32[2,768,384]{2,1,0:T(8,128)} %get-tuple-element.22) | copy-start | bytes 7077892
  166.9 2.5 %copy-start = (f32[2,384,768]{2,1,0:T(8,128)S(1)}, f32[2,384,768]{2,1,0:T(8,128)}, u32[]{:S(2)}) copy-start(f32[2,384,768]{2,1,0:T(8,128)} %get-tuple-element.23) | copy-start | bytes 7077892

commit v4 on v2

--- a/solution.py
+++ b/solution.py
@@ -67,9 +67,16 @@
     w_in_grad_hbm,
     w_out_grad_hbm,
     router_total,
+    raw,
     held,
     w_in,
     w_out,
+    mate_in,
+    mate_out,
+    give_in,
+    give_out,
+    took_in,
+    took_out,
     router_got,
     router,
     dispatch,
@@ -83,16 +90,15 @@
     act,
     slope,
     pre_grad,
-    cross,
     far,
     near,
+    aside,
     over,
     ready,
     back,
     combine_term,
     w_in_grad,
     w_out_grad,
-    result,
     router_message,
     router_first,
     router_mine,
@@ -100,30 +106,31 @@
     local,
     a2a_send,
     a2a_recv,
+    swap_send,
+    swap_recv,
     ag_send,
     ag_recv,
+    ag_far,
     rs_send,
-    cross_recv,
     far_recv,
     near_recv,
+    aside_recv,
     over_recv,
 ):
     dp, ex = lax.axis_index("dp"), lax.axis_index("expert")
     shards = 2 * RING
     x, z = lax.rem(dp, RING), dp // RING
-    x_right, x_left = lax.rem(x + 1, RING), lax.rem(x + 3, RING)
-    x_far = lax.rem(x + 2, RING)
-    other = 1 - z
-    partner = (other * RING + x, ex)
-    right = (z * RING + x_right, ex)
-    left = (z * RING + x_left, ex)
-    own = dp
-    mate = other * RING + x
+    odd = lax.rem(x, 2)
+    partner = ((1 - z) * RING + x, ex)
+    right = (z * RING + lax.rem(x + 1, RING), ex)
+    left = (z * RING + lax.rem(x + 3, RING), ex)
+    across = (z * RING + lax.rem(x + 1 + 2 * odd, RING), ex)
+    beside = (z * RING + lax.rem(x + 3 + 2 * odd, RING), ex)
     n_rows = experts * images
     half = rows.shape[-1] // 2
     slots = 2 * experts
     pairs = images * slots
-    n_tokens, n_padded = tokens_hbm.shape[0], held.shape[1]
+    n_tokens, n_padded = tokens_hbm.shape[0] * images, held.shape[1]
     chunks = rows.shape[-1] // LANES
     inner = experts // Z_HIGH
     lane = lax.rem(ex, inner)
@@ -134,8 +141,8 @@
         pltpu.make_async_copy(src, dst, local.at[k])
         for k, (src, dst) in enumerate(
             (
-                (tokens_hbm, held.at[0, pl.ds(0, n_tokens)]),
-                (cotangent_hbm, held.at[1, pl.ds(0, n_tokens)]),
+                (tokens_hbm, raw.at[0]),
+                (cotangent_hbm, raw.at[1]),
                 (w_in_hbm, w_in),
                 (w_out_hbm, w_out),
             )
@@ -161,7 +168,24 @@
     greeted = (Z_HIGH + 1) * inner
     lax.fori_loop(1, greeted, greet_experts, 0)
     lax.fori_loop(1, shards, greet_shards, 0)
+    for k in range(2):
+        loads[k].wait()
+        held[k, :n_tokens] = raw[k].reshape(n_tokens, held.shape[2])
+        if n_padded > n_tokens:
+            held[k, n_tokens:] = jnp.zeros((n_padded - n_tokens, held.shape[2]), LOW)
     pl.semaphore_wait(barrier, greeted - 1 + shards - 1)
+
+    for load in loads[2:]:
+        load.wait()
+    swap_with = (partner, across)
+
+    def swap(e, k, src, dst):
+        sent.append(remote(src, dst, swap_send.at[e, k], swap_recv.at[e, k], swap_with[e]))
+
+    sent = []
+    swap(1, 0, w_in.at[1], mate_in.at[1])
+    swap(0, 0, w_in.at[0], mate_in.at[0])
+    swap(1, 1, w_out.at[1], mate_out.at[1])
 
     def deliver(src, dst, k):
         def one(i, carry):
@@ -244,11 +268,6 @@
 
     collect(lambda block: router_own, router_got, 4)
     router_got[ex] = router_own[...]
-    for load in loads[:2]:
-        load.wait()
-    if n_padded > n_tokens:
-        for k in range(2):
-            held[k, n_tokens:] = jnp.zeros((n_padded - n_tokens, held.shape[2]), LOW)
     received(router_got, 4)
     flat = router_got[...].reshape(experts * CHUNK, LANES)
     away = distance((slots, experts * CHUNK), 1, by_slot)
@@ -294,144 +313,134 @@
         received(got.at[a], a)
         for h, block in enumerate(unpack(got[a], by_expert, 2 * n_rows)):
             for e in range(2):
-                rows[a, e, own, :, h * half : (h + 1) * half] = block[e * n_rows : (e + 1) * n_rows]
-
-    sent = []
-
-    def send_block(a, e, p, to, slot):
-        block = rows.at[a, e, p]
-        sent.append(remote(block, block, ag_send.at[a, slot], ag_recv.at[a, e, p], to))
-
-    def arrived(a, e, p):
-        await_bytes(rows.at[a, e, p], ag_recv.at[a, e, p])
+                rows[a, e, 0, :, h * half : (h + 1) * half] = block[e * n_rows : (e + 1) * n_rows]
+
+    bands = (pl.ds(0, n_rows // 2), pl.ds(n_rows // 2, n_rows // 2))
+    onward = (right, left)
+
+    def send_block(a, e, src, dst, to, slot):
+        sent.append(
+            remote(rows.at[a, e, src], rows.at[a, e, dst], ag_send.at[a, slot], ag_recv.at[a, e, dst], to)
+        )
+
+    def arrived(a, e, j):
+        await_bytes(rows.at[a, e, j], ag_recv.at[a, e, j])
 
     def gather_own(a):
-        for e in range(2):
-            send_block(a, e, own, partner, 3 * e)
-            send_block(a, e, own, right, 3 * e + 1)
-            send_block(a, e, own, left, 3 * e + 2)
+        send_block(a, 1, 0, 1, partner, 0)
+        send_block(a, 0, 0, 3, right, 1)
+        send_block(a, 0, 0, 1, left, 2)
+        send_block(a, 1, 0, 2, beside, 3)
 
     def gather_mate(a):
-        for e in range(2):
-            arrived(a, e, mate)
-            send_block(a, e, mate, right, 6 + 2 * e)
-            send_block(a, e, mate, left, 7 + 2 * e)
+        arrived(a, 1, 1)
+        send_block(a, 1, 1, 3, beside, 4)
 
     def gather_far(a):
-        for e, p, to in ((0, z * RING + x_left, right), (1, z * RING + x_right, left)):
-            arrived(a, e, p)
-            send_block(a, e, p, to, 10 + e)
-
-    def gather_cross(a):
-        for e in range(2):
-            arrived(a, e, z * RING + x_far)
-            send_block(a, e, z * RING + x_far, partner, 12 + e)
-
-    def near_rest(a):
-        arrived(a, 1, z * RING + x_left)
-        arrived(a, 0, z * RING + x_right)
-
-    def near_other(a):
-        for e in range(2):
-            arrived(a, e, other * RING + x_left)
-            arrived(a, e, other * RING + x_right)
-
-    def cross_rest(a):
-        for e in range(2):
-            arrived(a, e, other * RING + x_far)
-
-    def forward(e, p):
-        pre = dot(rows[0, e, p], w_in[e])
-        value, grade = gelu_and_slope(pre)
-        value = value.astype(LOW)
-        act[e, p] = value
-        slope[e, p] = grade
-        part[0, e, p] = dot(value, w_out[e]).astype(LOW)
-
-    def backward(e, p):
-        grad = turn(rows[1, e, p], w_out[e])
-        grad = (grad * slope[e, p]).astype(LOW)
-        pre_grad[e, p] = grad
-        part[1, e, p] = turn(grad, w_in[e]).astype(LOW)
-
-    def over_near(step, ring):
-        def one(k, carry):
-            step(lax.rem(k, 2), ring * RING + lax.rem(x + 1 + 2 * (k // 2), RING))
+        for side, j in enumerate((3, 1)):
+            arrived(a, 0, j)
+            sent.append(
+                remote(
+                    rows.at[a, 0, j, bands[side]],
+                    rows.at[a, 0, 2, bands[side]],
+                    ag_send.at[a, 5 + side],
+                    ag_far.at[a, side],
+                    onward[side],
+                )
+            )
+
+    def far_rest(a):
+        for side in range(2):
+            await_bytes(rows.at[a, 0, 2, bands[side]], ag_far.at[a, side])
+
+    def hidden(e):
+        return ((w_in.at[e], w_out.at[e]), (mate_in.at[e], mate_out.at[e]))
+
+    def forward(e, j):
+        total = 0.0
+        for h, (first, second) in enumerate(hidden(e)):
+            value, grade = gelu_and_slope(dot(rows[0, e, j], first[...]))
+            value = value.astype(LOW)
+            act[e, h, j] = value
+            slope[e, h, j] = grade
+            total = total + dot(value, second[...])
+        part[0, e, j] = total.astype(LOW)
+
+    def backward(e, j):
+        total = 0.0
+        for h, (first, second) in enumerate(hidden(e)):
+            grad = turn(rows[1, e, j], second[...])
+            grad = (grad * slope[e, h, j]).astype(LOW)
+            pre_grad[e, h, j] = grad
+            total = total + turn(grad, first[...])
+        part[1, e, j] = total.astype(LOW)
+
+    def several(step, e, start, stop):
+        def one(j, carry):
+            step(e, j)
             return carry
 
-        lax.fori_loop(0, 4, one, 0)
-
-    def over_experts(step, p):
-        def one(e, carry):
-            step(e, p)
-            return carry
-
-        lax.fori_loop(0, 2, one, 0)
-
-    def send_part(a, e, p, buffer, slot, recv, to):
-        sent.append(remote(part.at[a, e, p], buffer, rs_send.at[a, slot], recv, to))
-
-    def add(a, e, p, buffer, recv):
-        await_bytes(buffer, recv)
-        total = part[a, e, p].astype(SINGLE) + buffer[...].astype(SINGLE)
-        part[a, e, p] = total.astype(LOW)
-
-    def reduce_cross(a):
-        for e in range(2):
-            p = other * RING + x_far
-            send_part(a, e, p, cross.at[a, e], e, cross_recv.at[a, e], partner)
+        lax.fori_loop(start, stop, one, 0)
+
+    def send_part(src, dst, send, recv, to):
+        sent.append(remote(src, dst, send, recv, to))
 
     def reduce_far(a):
-        for e, to in ((0, right), (1, left)):
-            p = z * RING + x_far
-            add(a, e, p, cross.at[a, e], cross_recv.at[a, e])
-            send_part(a, e, p, far.at[a, e], 2 + e, far_recv.at[a, e], to)
-
-    def send_near(a, e, ring, which, side):
+        for side in range(2):
+            send_part(
+                part.at[a, 0, 2, bands[side]],
+                far.at[a, side],
+                rs_send.at[a, side],
+                far_recv.at[a, side],
+                onward[side],
+            )
+
+    def send_near(a, side, band):
         send_part(
-            a,
-            e,
-            ring * RING + (x_right, x_left)[side],
-            near.at[a, side, e, which],
-            4 + 4 * side + 2 * which + e,
-            near_recv.at[a, side, e, which],
-            (right, left)[side],
+            part.at[a, 0, (1, 3)[side], bands[band]],
+            near.at[a, side, bands[band]],
+            rs_send.at[a, 2 + 2 * side + band],
+            near_recv.at[a, side, band],
+            onward[side],
         )
 
-    def reduce_near_free(a):
-        for e in range(2):
-            for side in range(2):
-                send_near(a, e, other, 1, side)
-        for e in range(2):
-            send_near(a, e, z, 0, 1 - e)
-
-    def reduce_near(a):
-        for e in range(2):
-            add(a, e, z * RING + (x_right, x_left)[e], far.at[a, e], far_recv.at[a, e])
-            send_near(a, e, z, 0, e)
-
-    def near_total(a, e, ring, which):
+    def near_free(a):
         for side in range(2):
-            await_bytes(near.at[a, side, e, which], near_recv.at[a, side, e, which])
-        return (
-            part[a, e, ring * RING + x].astype(SINGLE)
-            + near[a, 0, e, which].astype(SINGLE)
-            + near[a, 1, e, which].astype(SINGLE)
-        )
+            send_near(a, side, 1 - side)
+
+    def near_summed(a):
+        for side in range(2):
+            j = (1, 3)[side]
+            await_bytes(far.at[a, side], far_recv.at[a, side])
+            total = part[a, 0, j, bands[side]].astype(SINGLE) + far[a, side].astype(SINGLE)
+            part[a, 0, j, bands[side]] = total.astype(LOW)
+            send_near(a, side, side)
+
+    def reduce_beside(a):
+        for k in (1, 0):
+            send_part(
+                part.at[a, 1, 2 + k], aside.at[a, k], rs_send.at[a, 6 + k], aside_recv.at[a, k], beside
+            )
+
+    def aside_total(a, k):
+        await_bytes(aside.at[a, k], aside_recv.at[a, k])
+        return part[a, 1, k].astype(SINGLE) + aside[a, k].astype(SINGLE)
 
     def reduce_over(a):
-        for e in range(2):
-            part[a, e, mate] = near_total(a, e, other, 1).astype(LOW)
-            send_part(a, e, mate, over.at[a, e], 12 + e, over_recv.at[a, e], partner)
+        part[a, 1, 1] = aside_total(a, 1).astype(LOW)
+        send_part(part.at[a, 1, 1], over.at[a], rs_send.at[a, 8], over_recv.at[a], partner)
 
     def give_back(a):
-        halves = ([], [])
-        for e in range(2):
-            total = near_total(a, e, z, 0)
-            await_bytes(over.at[a, e], over_recv.at[a, e])
-            total = (total + over[a, e].astype(SINGLE)).astype(LOW)
-            halves[0].append(total)
-        ready[a] = pack(jnp.concatenate(halves[0], axis=0), by_expert)
+        first = part[a, 0, 0].astype(SINGLE)
+        for side in range(2):
+            for band in range(2):
+                await_bytes(near.at[a, side, bands[band]], near_recv.at[a, side, band])
+            first = first + near[a, side].astype(SINGLE)
+        second = aside_total(a, 0)
+        await_bytes(over.at[a], over_recv.at[a])
+        second = second + over[a].astype(SINGLE)
+        total = jnp.concatenate([first.astype(LOW), second.astype(LOW)], axis=0)
+        ready[a] = pack(total, by_expert)
         collect(lambda block: ready.at[a, block], back.at[a], 2 + a)
         back[a, ex] = ready[a, lane]
 
@@ -446,68 +455,81 @@
         copy.start()
         stores.append(copy)
 
+    def flat(value):
+        return value.reshape(value.shape[0] * value.shape[1], value.shape[2])
+
     def weights(e):
-        def flat(value):
-            return value.reshape(value.shape[0] * value.shape[1], value.shape[2])
-
-        w_out_grad[e] = outer(flat(act[e]), flat(rows[1, e]))
-        w_in_grad[e] = outer(flat(rows[0, e]), flat(pre_grad[e]))
+        give_out[e] = outer(flat(act[e, 1]), flat(rows[1, e])).astype(LOW)
+        give_in[e] = outer(flat(rows[0, e]), flat(pre_grad[e, 1])).astype(LOW)
+        w_out_grad[e] = outer(flat(act[e, 0]), flat(rows[1, e]))
+        w_in_grad[e] = outer(flat(rows[0, e]), flat(pre_grad[e, 0]))
+
+    def weights_given(e):
+        swap(e, 2, give_out.at[e], took_out.at[e])
+        swap(e, 3, give_in.at[e], took_in.at[e])
+
+    def weights_taken(e):
+        await_bytes(took_out.at[e], swap_recv.at[e, 2])
+        w_out_grad[e] = w_out_grad[e] + took_out[e].astype(SINGLE)
         store(w_out_grad.at[e], w_out_grad_hbm.at[e], 4 + e)
+        await_bytes(took_in.at[e], swap_recv.at[e, 3])
+        w_in_grad[e] = w_in_grad[e] + took_in[e].astype(SINGLE)
         store(w_in_grad.at[e], w_in_grad_hbm.at[e], 6 + e)
+
+    def weights_here(e):
+        await_bytes(mate_in.at[e], swap_recv.at[e, 0])
+        await_bytes(mate_out.at[e], swap_recv.at[e, 1])
 
     own_rows(0)
     gather_own(0)
     deliver(message.at[1], got.at[1], 1)
-    for load in loads[2:]:
-        load.wait()
-    over_experts(forward, own)
+    swap(0, 1, w_out.at[0], mate_out.at[0])
     gather_mate(0)
+    weights_here(1)
+    forward(1, 0)
     gather_far(0)
-    over_experts(forward, mate)
+    forward(1, 1)
     own_rows(1)
     gather_own(1)
-    near_rest(0)
-    over_near(forward, z)
-    gather_cross(0)
-    over_experts(forward, z * RING + x_far)
-    near_other(0)
-    over_near(forward, other)
+    for j in (2, 3):
+        arrived(0, 1, j)
+    several(forward, 1, 2, 4)
     gather_mate(1)
     gather_far(1)
-    reduce_near_free(0)
-    cross_rest(0)
-    over_experts(forward, other * RING + x_far)
-    reduce_cross(0)
-    over_experts(backward, own)
-    over_experts(backward, mate)
-    near_rest(1)
-    over_near(backward, z)
-    gather_cross(1)
+    reduce_beside(0)
+    weights_here(0)
+    far_rest(0)
+    several(forward, 0, 0, 4)
     reduce_far(0)
-    over_experts(backward, z * RING + x_far)
-    near_other(1)
-    over_near(backward, other)
-    reduce_near(0)
-    reduce_near_free(1)
+    near_free(0)
     reduce_over(0)
-    cross_rest(1)
-    over_experts(backward, other * RING + x_far)
-    reduce_cross(1)
+    several(backward, 1, 0, 2)
+    for j in (2, 3):
+        arrived(1, 1, j)
+    several(backward, 1, 2, 4)
+    reduce_beside(1)
+    near_summed(0)
+    far_rest(1)
+    several(backward, 0, 0, 4)
+    reduce_far(1)
+    near_free(1)
+    reduce_over(1)
     give_back(0)
+    near_summed(1)
+    weights(1)
+    weights_given(1)
+    give_back(1)
     weights(0)
-    reduce_far(1)
-    reduce_over(1)
-    weights(1)
-    reduce_near(1)
+    weights_given(0)
 
     slot_out = given(0)
-    result[0] = outer(combine_low[...], slot_out)[:n_tokens].astype(LOW)
-    store(result.at[0], mixed_hbm, 8)
+    value = outer(combine_low[...], slot_out)[:n_tokens].astype(LOW)
+    raw[0] = value.reshape(raw.shape[1:])
+    store(raw.at[0], mixed_hbm, 8)
     grad = together(turn(slot_out, held[1]))
     weight = combine[...]
     combine_term[...] = weight * (grad - jnp.sum(weight * grad, axis=0, keepdims=True))
 
-    give_back(1)
     input_slots = given(1)
     grad = together(turn(input_slots, held[0]))
     weight = dispatch[...]
@@ -521,8 +543,8 @@
     router_message[...] = block.astype(LOW).reshape(experts, CHUNK, LANES)
     deliver(router_message, router_first, 5)
     value = outer(dispatch_low[...], input_slots) + outer(grad, router[...])
-    result[1] = value[:n_tokens].astype(LOW)
-    store(result.at[1], tokens_grad_hbm, 9)
+    raw[1] = value[:n_tokens].astype(LOW).reshape(raw.shape[1:])
+    store(raw.at[1], tokens_grad_hbm, 9)
 
     received(router_first, 5)
     router_mine[...] = jnp.sum(router_first[...].astype(SINGLE), axis=0)
@@ -543,6 +565,8 @@
     await_bytes(router_second.at[pl.ds(0, shards - 1)], a2a_recv.at[6])
     router_total[...] = jnp.sum(router_second[...], axis=0)
 
+    for e in (1, 0):
+        weights_taken(e)
     for k in range(4):
         await_bytes(got.at[0, pl.ds(0, experts - 1)], a2a_send.at[k])
     for k in range(4, 6):
@@ -565,11 +589,8 @@
     used = d * owned // LANES
     half = d // 2
 
-    def flat(value):
-        return value.transpose(1, 0, 2).reshape(n_tokens, d)
-
-    def unflat(value):
-        return value.reshape(n, images, d).transpose(1, 0, 2)
+    def swap(value):
+        return value.transpose(1, 0, 2)
 
     def low(*shape):
         return pltpu.VMEM(shape, LOW)
@@ -584,8 +605,8 @@
     mixed, tokens_grad, w_in_grad, w_out_grad, router_total = pl.pallas_call(
         functools.partial(layer_kernel, experts, images),
         out_shape=[
-            jax.ShapeDtypeStruct((n_tokens, d), LOW),
-            jax.ShapeDtypeStruct((n_tokens, d), LOW),
+            jax.ShapeDtypeStruct((n, images, d), LOW),
+            jax.ShapeDtypeStruct((n, images, d), LOW),
             jax.ShapeDtypeStruct(w_in.shape, SINGLE),
             jax.ShapeDtypeStruct(w_out.shape, SINGLE),
             jax.ShapeDtypeStruct((CHUNK, LANES), SINGLE),
@@ -593,7 +614,14 @@
         in_specs=[anywhere, anywhere, vmem, anywhere, anywhere],
         out_specs=[anywhere] * 4 + [vmem],
         scratch_shapes=[
+            low(2, n, images, d),
             low(2, n_padded, d),
+            low(*w_in.shape),
+            low(*w_out.shape),
+            low(*w_in.shape),
+            low(*w_out.shape),
+            low(*w_in.shape),
+            low(*w_out.shape),
             low(*w_in.shape),
             low(*w_out.shape),
             low(experts, CHUNK, LANES),
@@ -604,21 +632,20 @@
             low(images * slots, n_padded),
             low(2, experts, 4 * images, half),
             low(2, experts, 4 * images, half),
-            low(2, 2, 2 * RING, n_rows, d),
-            low(2, 2, 2 * RING, n_rows, d),
-            low(2, 2 * RING, n_rows, hidden),
-            single(2, 2 * RING, n_rows, hidden),
-            low(2, 2 * RING, n_rows, hidden),
+            low(2, 2, RING, n_rows, d),
+            low(2, 2, RING, n_rows, d),
+            low(2, 2, RING, n_rows, hidden),
+            single(2, 2, RING, n_rows, hidden),
+            low(2, 2, RING, n_rows, hidden),
+            low(2, 2, n_rows // 2, d),
             low(2, 2, n_rows, d),
             low(2, 2, n_rows, d),
-            low(2, 2, 2, 2, n_rows, d),
-            low(2, 2, n_rows, d),
+            low(2, n_rows, d),
             low(2, experts, 4 * images, half),
             low(2, experts, 4 * images, half),
             single(slots, n_padded),
             single(*w_in.shape),
             single(*w_out.shape),
-            low(2, n_tokens, d),
             low(experts, CHUNK, LANES),
             low(experts, CHUNK, LANES),
             single(CHUNK, LANES),
@@ -626,21 +653,24 @@
             dma((10,)),
             dma((7,)),
             dma((7,)),
-            dma((2, 14)),
-            dma((2, 2, 2 * RING)),
-            dma((2, 14)),
+            dma((2, 4)),
+            dma((2, 4)),
+            dma((2, 7)),
+            dma((2, 2, RING)),
             dma((2, 2)),
+            dma((2, 9)),
             dma((2, 2)),
-            dma((2, 2, 2, 2)),
+            dma((2, 2, 2)),
             dma((2, 2)),
+            dma((2,)),
         ],
         compiler_params=pltpu.CompilerParams(
             collective_id=0, has_side_effects=True, vmem_limit_bytes=58 * 1024 * 1024
         ),
         name="layer",
-    )(flat(tokens), flat(cotangent), router_own, w_in, w_out)
+    )(swap(tokens), swap(cotangent), router_own, w_in, w_out)
     router_grad = router_total[:used].reshape(owned, d).T
-    return (unflat(mixed), unflat(tokens_grad), w_in_grad, w_out_grad, router_grad)
+    return (swap(mixed), swap(tokens_grad), w_in_grad, w_out_grad, router_grad)
 
 
 def solution(mesh):

time: 174 us -> 156 us (0.90)
  Pallas kernels: 156 us -> 144 us
  local copies, waits for them, and re-layouts: 17.1 us -> 11.4 us
    pallas_call x1, Pallas kernels: 156 us -> 144 us  [body(): pl.pallas_call(functools.partial(layer_kernel, experts, images), out_shap...]
    reshape x4 -> x0, local copies, waits for them, and re-layouts: 11.3 us -> none  [the longest x2 6.79 us: unflat(): return value.reshape(n, images, d).transpose(1, 0, 2)]
    unnamed x10, local copies, waits for them, and re-layouts: 3.93 us -> 8.84 us
where the time goes in v4:
time: 156 us
  Pallas kernels  144 us (92%)
  local copies, waits for them, and re-layouts  11.4 us (7%)
    pallas_call x1, Pallas kernels, body(): pl.pallas_call(functools.partial(layer_kernel, experts, images), out_shap...  144 us
    unnamed x10, local copies, waits for them, and re-layouts  8.84 us

profile of v4, /device:TPU:1, one launch (start us, length us, event | category | flops | bytes accessed | tf_op | source)
XLA Modules:
  0.0 155.6 jit_solution(10864039597274344239)
XLA Ops:
  0.6 0.7 reshape.16
  1.3 0.6 pad.4.router_own
  1.9 143.5 %layer.1 = (bf16[196,4,768]{2,1,0:T(4,128)(2,1)}, bf16[196,4,768]{2,1,0:T(4,128)(2,1)}, f32[2,768,384]{2,1,0:T(8,128)}, f32[2,384,768]{2,1,0:T(8,128)}, f32[16,128]{1,0:T(8,128)}) custom-call(bf16[196,4,768]{2,1,0:T(4,128)(2,1)} %bitcast.9, bf16[196,4,768]{2,1,0:T(4,128)(2,1)} %bitcast.10, bf16[16,128]{1,0:T(8,128)(2,1)} %pad.4.router_own, ...), custom_call_target="tpu_custom_call" | custom-call | tf_op jit(solution)/shard_map/layer/pallas_call | solution.py:605
  145.5 1.3 reshape.17
  146.8 0.0 copy-start.2
  146.8 2.8 %copy.14 = bf16[4,196,768]{2,0,1:T(4,128)(2,1)} copy(bf16[4,196,768]{2,0,1:T(4,128)(2,1)} %bitcast.8) | data formatting | bytes 2408448
  149.6 0.0 copy-done.2
  149.6 0.0 copy-start.1
  149.6 1.0 copy.15
  150.6 1.1 copy-done.1
  151.7 0.0 copy-start
  151.7 1.4 copy.16
  153.1 1.1 copy-done
  154.2 1.4 copy.17
Async XLA Ops:
  146.8 2.8 %copy-start.2 = (bf16[196,4,768]{2,1,0:T(4,128)(2,1)S(1)}, bf16[196,4,768]{2,1,0:T(4,128)(2,1)}, u32[]{:S(2)}) copy-start(bf16[196,4,768]{2,1,0:T(4,128)(2,1)} %get-tuple-element.11) | copy-start | bytes 3612676
  149.6 2.1 %copy-start.1 = (f32[2,768,384]{2,1,0:T(8,128)S(1)}, f32[2,768,384]{2,1,0:T(8,128)}, u32[]{:S(2)}) copy-start(f32[2,768,384]{2,1,0:T(8,128)} %get-tuple-element.22) | copy-start | bytes 7077892
  151.7 2.5 %copy-start = (f32[2,384,768]{2,1,0:T(8,128)S(1)}, f32[2,384,768]{2,1,0:T(8,128)}, u32[]{:S(2)}) copy-start(f32[2,384,768]{2,1,0:T(8,128)} %get-tuple-element.23) | copy-start | bytes 7077892

commit v5 on v4

--- a/solution.py
+++ b/solution.py
@@ -13,6 +13,8 @@
 RING = 4
 Z_HIGH = 4
 LANES = 128
+VMEM_BYTES = 58 * 1024 * 1024
+PARTS = 4
 CHUNK = 16
 
 
@@ -59,14 +61,14 @@
     images,
     tokens_hbm,
     cotangent_hbm,
-    router_own,
+    router_columns,
     w_in_hbm,
     w_out_hbm,
     mixed_hbm,
     tokens_grad_hbm,
     w_in_grad_hbm,
     w_out_grad_hbm,
-    router_total,
+    router_grad,
     raw,
     held,
     w_in,
@@ -77,6 +79,7 @@
     give_out,
     took_in,
     took_out,
+    router_own,
     router_got,
     router,
     dispatch,
@@ -92,6 +95,7 @@
     pre_grad,
     far,
     near,
+    cross,
     aside,
     over,
     ready,
@@ -114,6 +118,7 @@
     rs_send,
     far_recv,
     near_recv,
+    cross_recv,
     aside_recv,
     over_recv,
 ):
@@ -150,6 +155,11 @@
     ]
     for load in loads:
         load.start()
+    owned = router_columns.shape[0]
+    value = router_columns[...].astype(SINGLE)
+    lines = [value[s : s + 1, c * LANES : (c + 1) * LANES] for s in range(owned) for c in range(chunks)]
+    lines.append(jnp.zeros((CHUNK - owned * chunks, LANES), SINGLE))
+    router_own[...] = jnp.concatenate(lines, axis=0).astype(LOW)
 
     barrier = pltpu.get_barrier_semaphore()
 
@@ -168,11 +178,14 @@
     greeted = (Z_HIGH + 1) * inner
     lax.fori_loop(1, greeted, greet_experts, 0)
     lax.fori_loop(1, shards, greet_shards, 0)
-    for k in range(2):
+
+    def hold(k):
         loads[k].wait()
         held[k, :n_tokens] = raw[k].reshape(n_tokens, held.shape[2])
         if n_padded > n_tokens:
             held[k, n_tokens:] = jnp.zeros((n_padded - n_tokens, held.shape[2]), LOW)
+
+    hold(0)
     pl.semaphore_wait(barrier, greeted - 1 + shards - 1)
 
     for load in loads[2:]:
@@ -303,6 +316,7 @@
     apart(weight, dispatch_low)
     message[0] = pack(dot(dispatch_low[...], held[0]).astype(LOW), by_image)
     deliver(message.at[0], got.at[0], 0)
+    hold(1)
     weight = jnp.exp(logits - jnp.max(logits, axis=0, keepdims=True))
     weight = weight / jnp.sum(weight, axis=0, keepdims=True)
     combine[...] = weight
@@ -416,19 +430,15 @@
             part[a, 0, j, bands[side]] = total.astype(LOW)
             send_near(a, side, side)
 
+    def reduce_cross(a):
+        send_part(part.at[a, 1, 3], cross.at[a], rs_send.at[a, 6], cross_recv.at[a], partner)
+        send_part(part.at[a, 1, 1], over.at[a], rs_send.at[a, 7], over_recv.at[a], partner)
+
     def reduce_beside(a):
-        for k in (1, 0):
-            send_part(
-                part.at[a, 1, 2 + k], aside.at[a, k], rs_send.at[a, 6 + k], aside_recv.at[a, k], beside
-            )
-
-    def aside_total(a, k):
-        await_bytes(aside.at[a, k], aside_recv.at[a, k])
-        return part[a, 1, k].astype(SINGLE) + aside[a, k].astype(SINGLE)
-
-    def reduce_over(a):
-        part[a, 1, 1] = aside_total(a, 1).astype(LOW)
-        send_part(part.at[a, 1, 1], over.at[a], rs_send.at[a, 8], over_recv.at[a], partner)
+        await_bytes(cross.at[a], cross_recv.at[a])
+        total = part[a, 1, 2].astype(SINGLE) + cross[a].astype(SINGLE)
+        part[a, 1, 2] = total.astype(LOW)
+        send_part(part.at[a, 1, 2], aside.at[a], rs_send.at[a, 8], aside_recv.at[a], beside)
 
     def give_back(a):
         first = part[a, 0, 0].astype(SINGLE)
@@ -436,9 +446,9 @@
             for band in range(2):
                 await_bytes(near.at[a, side, bands[band]], near_recv.at[a, side, band])
             first = first + near[a, side].astype(SINGLE)
-        second = aside_total(a, 0)
+        await_bytes(aside.at[a], aside_recv.at[a])
         await_bytes(over.at[a], over_recv.at[a])
-        second = second + over[a].astype(SINGLE)
+        second = part[a, 1, 0].astype(SINGLE) + aside[a].astype(SINGLE) + over[a].astype(SINGLE)
         total = jnp.concatenate([first.astype(LOW), second.astype(LOW)], axis=0)
         ready[a] = pack(total, by_expert)
         collect(lambda block: ready.at[a, block], back.at[a], 2 + a)
@@ -458,15 +468,17 @@
     def flat(value):
         return value.reshape(value.shape[0] * value.shape[1], value.shape[2])
 
-    def weights(e):
+    def weights_out(e):
         give_out[e] = outer(flat(act[e, 1]), flat(rows[1, e])).astype(LOW)
+        swap(e, 2, give_out.at[e], took_out.at[e])
+
+    def weights_in(e):
         give_in[e] = outer(flat(rows[0, e]), flat(pre_grad[e, 1])).astype(LOW)
+        swap(e, 3, give_in.at[e], took_in.at[e])
+
+    def weights_own(e):
         w_out_grad[e] = outer(flat(act[e, 0]), flat(rows[1, e]))
         w_in_grad[e] = outer(flat(rows[0, e]), flat(pre_grad[e, 0]))
-
-    def weights_given(e):
-        swap(e, 2, give_out.at[e], took_out.at[e])
-        swap(e, 3, give_in.at[e], took_in.at[e])
 
     def weights_taken(e):
         await_bytes(took_out.at[e], swap_recv.at[e, 2])
@@ -496,31 +508,33 @@
     several(forward, 1, 2, 4)
     gather_mate(1)
     gather_far(1)
-    reduce_beside(0)
+    reduce_cross(0)
     weights_here(0)
     far_rest(0)
     several(forward, 0, 0, 4)
     reduce_far(0)
     near_free(0)
-    reduce_over(0)
+    reduce_beside(0)
     several(backward, 1, 0, 2)
     for j in (2, 3):
         arrived(1, 1, j)
     several(backward, 1, 2, 4)
-    reduce_beside(1)
+    reduce_cross(1)
     near_summed(0)
     far_rest(1)
     several(backward, 0, 0, 4)
     reduce_far(1)
     near_free(1)
-    reduce_over(1)
+    reduce_beside(1)
+    near_summed(1)
     give_back(0)
-    near_summed(1)
-    weights(1)
-    weights_given(1)
+    weights_out(0)
     give_back(1)
-    weights(0)
-    weights_given(0)
+    weights_in(0)
+    weights_out(1)
+    weights_in(1)
+    weights_own(0)
+    weights_own(1)
 
     slot_out = given(0)
     value = outer(combine_low[...], slot_out)[:n_tokens].astype(LOW)
@@ -563,7 +577,11 @@
     lax.fori_loop(1, shards, share, 0)
     router_second[dp] = router_mine[...]
     await_bytes(router_second.at[pl.ds(0, shards - 1)], a2a_recv.at[6])
-    router_total[...] = jnp.sum(router_second[...], axis=0)
+    value = jnp.sum(router_second[...], axis=0)
+    for s in range(owned):
+        for c in range(chunks):
+            at = s * chunks + c
+            router_grad[s : s + 1, c * LANES : (c + 1) * LANES] = value[at : at + 1]
 
     for e in (1, 0):
         weights_taken(e)
@@ -578,6 +596,45 @@
         copy.wait()
 
 
+def finish_kernel(*refs):
+    count = (len(refs) - 2) // 3
+    sources, results, staged = (refs[k * count : (k + 1) * count] for k in range(3))
+    into, out = refs[-2:]
+    pieces = []
+    for src, dst, held in zip(sources, results, staged):
+        parts = 1 if len(src.shape) < 3 else PARTS if src.shape[0] % PARTS == 0 else src.shape[0]
+        size = src.shape[0] // parts
+        for at in range(parts):
+            rows, k = pl.ds(at * size, size), len(pieces)
+            pieces.append(
+                (
+                    pltpu.make_async_copy(src.at[rows], held.at[rows], into.at[k]),
+                    pltpu.make_async_copy(held.at[rows], dst.at[rows], out.at[k]),
+                )
+            )
+    for read, _ in pieces:
+        read.start()
+    for read, write in pieces:
+        read.wait()
+        write.start()
+    for _, write in pieces:
+        write.wait()
+
+
+def finish(*values):
+    anywhere = pl.BlockSpec(memory_space=pl.ANY)
+    return pl.pallas_call(
+        finish_kernel,
+        out_shape=[jax.ShapeDtypeStruct(value.shape, value.dtype) for value in values],
+        in_specs=[anywhere] * len(values),
+        out_specs=[anywhere] * len(values),
+        scratch_shapes=[pltpu.VMEM(value.shape, value.dtype) for value in values]
+        + [pltpu.SemaphoreType.DMA((PARTS * len(values),))] * 2,
+        compiler_params=pltpu.CompilerParams(vmem_limit_bytes=VMEM_BYTES),
+        name="finish",
+    )(*values)
+
+
 def body(experts, tokens, router, w_in, w_out, cotangent):
     images, n, d = tokens.shape
     hidden = w_in.shape[2]
@@ -586,7 +643,6 @@
     n_tokens = images * n
     n_padded = -(-n_tokens // LANES) * LANES
     n_rows = experts * images
-    used = d * owned // LANES
     half = d // 2
 
     def swap(value):
@@ -598,20 +654,20 @@
     def single(*shape):
         return pltpu.VMEM(shape, SINGLE)
 
-    router_own = jnp.pad(router.T.reshape(used, LANES), ((0, CHUNK - used), (0, 0)))
     anywhere = pl.BlockSpec(memory_space=pl.ANY)
+    in_hbm = pl.BlockSpec(memory_space=pltpu.HBM)
     vmem = pl.BlockSpec(memory_space=pltpu.VMEM)
     dma = pltpu.SemaphoreType.DMA
-    mixed, tokens_grad, w_in_grad, w_out_grad, router_total = pl.pallas_call(
+    mixed, tokens_grad, w_in_grad, w_out_grad, router_grad = pl.pallas_call(
         functools.partial(layer_kernel, experts, images),
         out_shape=[
             jax.ShapeDtypeStruct((n, images, d), LOW),
             jax.ShapeDtypeStruct((n, images, d), LOW),
             jax.ShapeDtypeStruct(w_in.shape, SINGLE),
             jax.ShapeDtypeStruct(w_out.shape, SINGLE),
-            jax.ShapeDtypeStruct((CHUNK, LANES), SINGLE),
+            jax.ShapeDtypeStruct((owned, d), SINGLE),
         ],
-        in_specs=[anywhere, anywhere, vmem, anywhere, anywhere],
+        in_specs=[in_hbm, in_hbm, vmem, in_hbm, in_hbm],
         out_specs=[anywhere] * 4 + [vmem],
         scratch_shapes=[
             low(2, n, images, d),
@@ -624,6 +680,7 @@
             low(*w_out.shape),
             low(*w_in.shape),
             low(*w_out.shape),
+            low(CHUNK, LANES),
             low(experts, CHUNK, LANES),
             low(slots, d),
             single(slots, n_padded),
@@ -639,7 +696,8 @@
             low(2, 2, RING, n_rows, hidden),
             low(2, 2, n_rows // 2, d),
             low(2, 2, n_rows, d),
-            low(2, 2, n_rows, d),
+            low(2, n_rows, d),
+            low(2, n_rows, d),
             low(2, n_rows, d),
             low(2, experts, 4 * images, half),
             low(2, experts, 4 * images, half),
@@ -661,16 +719,19 @@
             dma((2, 9)),
             dma((2, 2)),
             dma((2, 2, 2)),
-            dma((2, 2)),
+            dma((2,)),
+            dma((2,)),
             dma((2,)),
         ],
         compiler_params=pltpu.CompilerParams(
-            collective_id=0, has_side_effects=True, vmem_limit_bytes=58 * 1024 * 1024
+            collective_id=0, has_side_effects=True, vmem_limit_bytes=VMEM_BYTES
         ),
         name="layer",
-    )(swap(tokens), swap(cotangent), router_own, w_in, w_out)
-    router_grad = router_total[:used].reshape(owned, d).T
-    return (swap(mixed), swap(tokens_grad), w_in_grad, w_out_grad, router_grad)
+    )(swap(tokens), swap(cotangent), router.T, w_in, w_out)
+    mixed, tokens_grad, w_in_grad, w_out_grad, router_grad = finish(
+        mixed, tokens_grad, w_in_grad, w_out_grad, router_grad
+    )
+    return (swap(mixed), swap(tokens_grad), w_in_grad, w_out_grad, router_grad.T)
 
 
 def solution(mesh):

time: 156 us -> 137 us (0.88)
  local copies, waits for them, and re-layouts: 11.4 us -> 0 us
  Pallas kernels: 144 us -> 136 us
    pallas_call x1, Pallas kernels: 144 us -> 130 us  [body(): pl.pallas_call(functools.partial(layer_kernel, experts, images), out_shap...]
    unnamed x10 -> x0, local copies, waits for them, and re-layouts: 8.84 us -> none
    pallas_call x0 -> x1, Pallas kernels: none -> 6.02 us  [finish(): pl.pallas_call(finish_kernel, out_shape=[jax.ShapeDtypeStruct(value.shape...]
    reshape x2 -> x0, local copies, waits for them, and re-layouts: 2 us -> none  [the longest x1 1.3 us: body(): router_grad = router_total[:used].reshape(owned, d).T]
where the time goes in v5:
time: 137 us
  Pallas kernels  136 us (99%)
    pallas_call x1, Pallas kernels, body(): pl.pallas_call(functools.partial(layer_kernel, experts, images), out_shap...  130 us
    pallas_call x1, Pallas kernels, finish(): pl.pallas_call(finish_kernel, out_shape=[jax.ShapeDtypeStruct(value.shape...  6.02 us

profile of v5, /device:TPU:1, one launch (start us, length us, event | category | flops | bytes accessed | tf_op | source)
XLA Modules:
  0.0 136.9 jit_solution(12634907117825387489)
XLA Ops:
  0.6 130.1 %layer.1 = (bf16[196,4,768]{2,1,0:T(4,128)(2,1)}, bf16[196,4,768]{2,1,0:T(4,128)(2,1)}, f32[2,768,384]{2,1,0:T(8,128)}, f32[2,384,768]{2,1,0:T(8,128)}, f32[2,768]{1,0:T(2,128)}) custom-call(bf16[196,4,768]{2,1,0:T(4,128)(2,1)} %bitcast.6, bf16[196,4,768]{2,1,0:T(4,128)(2,1)} %bitcast.7, bf16[2,768]{1,0:T(2,128)(2,1)} %bitcast.8, ...), custom_call_target="tpu_custom_call" | custom-call | tf_op jit(solution)/shard_map/layer/pallas_call | solution.py:661
  130.7 6.0 %finish.1 = (bf16[196,4,768]{2,1,0:T(4,128)(2,1)}, bf16[196,4,768]{2,1,0:T(4,128)(2,1)}, f32[2,768,384]{2,1,0:T(8,128)}, f32[2,384,768]{2,1,0:T(8,128)}, f32[2,768]{1,0:T(2,128)}) custom-call(bf16[196,4,768]{2,1,0:T(4,128)(2,1)} %get-tuple-element.15.refs_0_, bf16[196,4,768]{2,1,0:T(4,128)(2,1)} %get-tuple-element.16.refs_1_, ...), custom_call_target="tpu_custom_call" | custom-call | tf_op jit(solution)/shard_map/finish/pallas_call | solution.py:626

commit v6 on v5

--- a/solution.py
+++ b/solution.py
@@ -49,11 +49,6 @@
 
 def dot(lhs, rhs):
     return jnp.dot(lhs, rhs, preferred_element_type=SINGLE)
-
-
-def place_of(z_at, lane, x, experts):
-    z_at = lax.rem(z_at + 4 * Z_HIGH, 2 * Z_HIGH)
-    return (lax.rem(z_at, 2) * RING + x, (z_at // 2) * (experts // Z_HIGH) + lane)
 
 
 def layer_kernel(
@@ -163,12 +158,25 @@
 
     barrier = pltpu.get_barrier_semaphore()
 
-    def greet_experts(k, carry):
-        step = k // inner
-        step = step - (step // Z_HIGH) * (Z_HIGH + 2)
-        to = place_of(z_at - step * way, lax.rem(lane + k, inner), x, experts)
-        pl.semaphore_signal(barrier, inc=1, device_id=to, device_id_type=MESH)
-        return carry
+    def each_lane(step, what):
+        def one(i, carry):
+            what(lax.rem(lane + i, inner))
+            return carry
+
+        lax.fori_loop(0 if step else 1, inner, one, 0, unroll=True)
+
+    def at_z(offset):
+        z_to = lax.rem(z_at + offset + 4 * Z_HIGH, 2 * Z_HIGH)
+        return lax.rem(z_to, 2) * RING + x, (z_to // 2) * inner
+
+    def greet_experts(step, offset):
+        dp_to, first = at_z(offset)
+
+        def one(there):
+            to = (dp_to, first + there)
+            pl.semaphore_signal(barrier, inc=1, device_id=to, device_id_type=MESH)
+
+        each_lane(step, one)
 
     def greet_shards(k, carry):
         to = (lax.rem(dp + k, shards), ex)
@@ -176,8 +184,9 @@
         return carry
 
     greeted = (Z_HIGH + 1) * inner
-    lax.fori_loop(1, greeted, greet_experts, 0)
-    lax.fori_loop(1, shards, greet_shards, 0)
+    for step, offset in enumerate((0, -way, -2 * way, -3 * way, 2 * way)):
+        greet_experts(step, offset)
+    lax.fori_loop(1, shards, greet_shards, 0, unroll=True)
 
     def hold(k):
         loads[k].wait()
@@ -191,6 +200,8 @@
     for load in loads[2:]:
         load.wait()
     swap_with = (partner, across)
+    some = w_out.shape[1] // 2
+    early, late = pl.ds(0, some), pl.ds(some, some)
 
     def swap(e, k, src, dst):
         sent.append(remote(src, dst, swap_send.at[e, k], swap_recv.at[e, k], swap_with[e]))
@@ -201,39 +212,37 @@
     swap(1, 1, w_out.at[1], mate_out.at[1])
 
     def deliver(src, dst, k):
-        def one(i, carry):
-            step = i // inner
-            to = place_of(
-                z_at + step * way * (1 - 2 * lax.rem(step, 2)), lax.rem(lane + i, inner), x, experts
-            )
-            pltpu.make_async_remote_copy(
-                src_ref=src.at[to[1]],
-                dst_ref=dst.at[step * inner + lane],
-                send_sem=a2a_send.at[k],
-                recv_sem=a2a_recv.at[k],
-                device_id=to,
-                device_id_type=MESH,
-            ).start()
-            return carry
-
-        lax.fori_loop(1, experts, one, 0)
+        for step in range(Z_HIGH):
+            dp_to, first = at_z(step * way * (1 - 2 * (step % 2)))
+
+            def one(there, step=step, dp_to=dp_to, first=first):
+                pltpu.make_async_remote_copy(
+                    src_ref=src.at[first + there],
+                    dst_ref=dst.at[step * inner + lane],
+                    send_sem=a2a_send.at[k],
+                    recv_sem=a2a_recv.at[k],
+                    device_id=(dp_to, first + there),
+                    device_id_type=MESH,
+                ).start()
+
+            each_lane(step, one)
         dst[lane] = src[ex]
 
     def collect(src_of, dst, k):
-        def one(i, carry):
-            step = i // inner
-            there = lax.rem(lane + i, inner)
-            pltpu.make_async_remote_copy(
-                src_ref=src_of(step * inner + there),
-                dst_ref=dst.at[ex],
-                send_sem=a2a_send.at[k],
-                recv_sem=a2a_recv.at[k],
-                device_id=place_of(z_at - step * way, there, x, experts),
-                device_id_type=MESH,
-            ).start()
-            return carry
-
-        lax.fori_loop(1, experts, one, 0)
+        for step in range(Z_HIGH):
+            dp_to, first = at_z(-step * way)
+
+            def one(there, step=step, dp_to=dp_to, first=first):
+                pltpu.make_async_remote_copy(
+                    src_ref=src_of(step * inner + there),
+                    dst_ref=dst.at[ex],
+                    send_sem=a2a_send.at[k],
+                    recv_sem=a2a_recv.at[k],
+                    device_id=(dp_to, first + there),
+                    device_id_type=MESH,
+                ).start()
+
+            each_lane(step, one)
 
     def received(ref, k):
         await_bytes(ref.at[pl.ds(0, experts - 1)], a2a_recv.at[k])
@@ -316,6 +325,7 @@
     apart(weight, dispatch_low)
     message[0] = pack(dot(dispatch_low[...], held[0]).astype(LOW), by_image)
     deliver(message.at[0], got.at[0], 0)
+    swap(0, 1, w_out.at[0, early], mate_out.at[0, early])
     hold(1)
     weight = jnp.exp(logits - jnp.max(logits, axis=0, keepdims=True))
     weight = weight / jnp.sum(weight, axis=0, keepdims=True)
@@ -490,12 +500,16 @@
 
     def weights_here(e):
         await_bytes(mate_in.at[e], swap_recv.at[e, 0])
-        await_bytes(mate_out.at[e], swap_recv.at[e, 1])
+        if e == 0:
+            await_bytes(mate_out.at[e, early], swap_recv.at[e, 1])
+            await_bytes(mate_out.at[e, late], swap_recv.at[e, 4])
+        else:
+            await_bytes(mate_out.at[e], swap_recv.at[e, 1])
 
     own_rows(0)
     gather_own(0)
     deliver(message.at[1], got.at[1], 1)
-    swap(0, 1, w_out.at[0], mate_out.at[0])
+    swap(0, 4, w_out.at[0, late], mate_out.at[0, late])
     gather_mate(0)
     weights_here(1)
     forward(1, 0)
@@ -525,13 +539,13 @@
     several(backward, 0, 0, 4)
     reduce_far(1)
     near_free(1)
-    reduce_beside(1)
+    weights_out(0)
     near_summed(1)
     give_back(0)
-    weights_out(0)
+    reduce_beside(1)
+    weights_out(1)
     give_back(1)
     weights_in(0)
-    weights_out(1)
     weights_in(1)
     weights_own(0)
     weights_own(1)
@@ -574,7 +588,7 @@
         ).start()
         return carry
 
-    lax.fori_loop(1, shards, share, 0)
+    lax.fori_loop(1, shards, share, 0, unroll=True)
     router_second[dp] = router_mine[...]
     await_bytes(router_second.at[pl.ds(0, shards - 1)], a2a_recv.at[6])
     value = jnp.sum(router_second[...], axis=0)
@@ -711,8 +725,8 @@
             dma((10,)),
             dma((7,)),
             dma((7,)),
-            dma((2, 4)),
-            dma((2, 4)),
+            dma((2, 5)),
+            dma((2, 5)),
             dma((2, 7)),
             dma((2, 2, RING)),
             dma((2, 2)),

time: 137 us -> 128 us (0.934)
  Pallas kernels: 136 us -> 127 us
    pallas_call x1, Pallas kernels: 130 us -> 121 us  [body(): pl.pallas_call(functools.partial(layer_kernel, experts, images), out_shap...]
where the time goes in v6:
time: 128 us
  Pallas kernels  127 us (99%)
    pallas_call x1, Pallas kernels, body(): pl.pallas_call(functools.partial(layer_kernel, experts, images), out_shap...  121 us
    pallas_call x1, Pallas kernels, finish(): pl.pallas_call(finish_kernel, out_shape=[jax.ShapeDtypeStruct(value.shape...  6.02 us

profile of v6, /device:TPU:1, one launch (start us, length us, event | category | flops | bytes accessed | tf_op | source)
XLA Modules:
  0.0 127.8 jit_solution(4557567769588811126)
XLA Ops:
  0.6 121.0 %layer.1 = (bf16[196,4,768]{2,1,0:T(4,128)(2,1)}, bf16[196,4,768]{2,1,0:T(4,128)(2,1)}, f32[2,768,384]{2,1,0:T(8,128)}, f32[2,384,768]{2,1,0:T(8,128)}, f32[2,768]{1,0:T(2,128)}) custom-call(bf16[196,4,768]{2,1,0:T(4,128)(2,1)} %bitcast.6, bf16[196,4,768]{2,1,0:T(4,128)(2,1)} %bitcast.7, bf16[2,768]{1,0:T(2,128)(2,1)} %bitcast.8, ...), custom_call_target="tpu_custom_call" | custom-call | tf_op jit(solution)/shard_map/layer/pallas_call | solution.py:675
  121.7 6.0 %finish.1 = (bf16[196,4,768]{2,1,0:T(4,128)(2,1)}, bf16[196,4,768]{2,1,0:T(4,128)(2,1)}, f32[2,768,384]{2,1,0:T(8,128)}, f32[2,384,768]{2,1,0:T(8,128)}, f32[2,768]{1,0:T(2,128)}) custom-call(bf16[196,4,768]{2,1,0:T(4,128)(2,1)} %get-tuple-element.15.refs_0_, bf16[196,4,768]{2,1,0:T(4,128)(2,1)} %get-tuple-element.16.refs_1_, ...), custom_call_target="tpu_custom_call" | custom-call | tf_op jit(solution)/shard_map/finish/pallas_call | solution.py:640

commit v7 on v6

--- a/solution.py
+++ b/solution.py
@@ -197,8 +197,6 @@
     hold(0)
     pl.semaphore_wait(barrier, greeted - 1 + shards - 1)
 
-    for load in loads[2:]:
-        load.wait()
     swap_with = (partner, across)
     some = w_out.shape[1] // 2
     early, late = pl.ds(0, some), pl.ds(some, some)
@@ -207,9 +205,6 @@
         sent.append(remote(src, dst, swap_send.at[e, k], swap_recv.at[e, k], swap_with[e]))
 
     sent = []
-    swap(1, 0, w_in.at[1], mate_in.at[1])
-    swap(0, 0, w_in.at[0], mate_in.at[0])
-    swap(1, 1, w_out.at[1], mate_out.at[1])
 
     def deliver(src, dst, k):
         for step in range(Z_HIGH):
@@ -289,6 +284,11 @@
         return [dot(mark(away, h * 2 * images), flat).astype(LOW) for h in range(2)]
 
     collect(lambda block: router_own, router_got, 4)
+    for load in loads[2:]:
+        load.wait()
+    swap(1, 0, w_in.at[1], mate_in.at[1])
+    swap(0, 0, w_in.at[0], mate_in.at[0])
+    swap(1, 1, w_out.at[1], mate_out.at[1])
     router_got[ex] = router_own[...]
     received(router_got, 4)
     flat = router_got[...].reshape(experts * CHUNK, LANES)
@@ -482,9 +482,14 @@
         give_out[e] = outer(flat(act[e, 1]), flat(rows[1, e])).astype(LOW)
         swap(e, 2, give_out.at[e], took_out.at[e])
 
+    third = w_in.shape[1] // 3
+    thirds = [pl.ds(k * third, third) for k in range(3)]
+
     def weights_in(e):
         give_in[e] = outer(flat(rows[0, e]), flat(pre_grad[e, 1])).astype(LOW)
-        swap(e, 3, give_in.at[e], took_in.at[e])
+
+    def weights_in_given(e, k):
+        swap(e, 4 + k, give_in.at[e, thirds[k]], took_in.at[e, thirds[k]])
 
     def weights_own(e):
         w_out_grad[e] = outer(flat(act[e, 0]), flat(rows[1, e]))
@@ -494,7 +499,8 @@
         await_bytes(took_out.at[e], swap_recv.at[e, 2])
         w_out_grad[e] = w_out_grad[e] + took_out[e].astype(SINGLE)
         store(w_out_grad.at[e], w_out_grad_hbm.at[e], 4 + e)
-        await_bytes(took_in.at[e], swap_recv.at[e, 3])
+        for k in range(3):
+            await_bytes(took_in.at[e, thirds[k]], swap_recv.at[e, 4 + k])
         w_in_grad[e] = w_in_grad[e] + took_in[e].astype(SINGLE)
         store(w_in_grad.at[e], w_in_grad_hbm.at[e], 6 + e)
 
@@ -502,14 +508,14 @@
         await_bytes(mate_in.at[e], swap_recv.at[e, 0])
         if e == 0:
             await_bytes(mate_out.at[e, early], swap_recv.at[e, 1])
-            await_bytes(mate_out.at[e, late], swap_recv.at[e, 4])
+            await_bytes(mate_out.at[e, late], swap_recv.at[e, 3])
         else:
             await_bytes(mate_out.at[e], swap_recv.at[e, 1])
 
     own_rows(0)
     gather_own(0)
     deliver(message.at[1], got.at[1], 1)
-    swap(0, 4, w_out.at[0, late], mate_out.at[0, late])
+    swap(0, 3, w_out.at[0, late], mate_out.at[0, late])
     gather_mate(0)
     weights_here(1)
     forward(1, 0)
@@ -546,7 +552,10 @@
     weights_out(1)
     give_back(1)
     weights_in(0)
+    weights_in_given(0, 0)
     weights_in(1)
+    for k in range(3):
+        weights_in_given(1, k)
     weights_own(0)
     weights_own(1)
 
@@ -570,6 +579,8 @@
     )
     router_message[...] = block.astype(LOW).reshape(experts, CHUNK, LANES)
     deliver(router_message, router_first, 5)
+    for k in (1, 2):
+        weights_in_given(0, k)
     value = outer(dispatch_low[...], input_slots) + outer(grad, router[...])
     raw[1] = value[:n_tokens].astype(LOW).reshape(raw.shape[1:])
     store(raw.at[1], tokens_grad_hbm, 9)
@@ -725,8 +736,8 @@
             dma((10,)),
             dma((7,)),
             dma((7,)),
-            dma((2, 5)),
-            dma((2, 5)),
+            dma((2, 7)),
+            dma((2, 7)),
             dma((2, 7)),
             dma((2, 2, RING)),
             dma((2, 2)),

time: 128 us -> 126 us (0.984)
  Pallas kernels: 127 us -> 125 us
    pallas_call x1, Pallas kernels: 121 us -> 119 us  [body(): pl.pallas_call(functools.partial(layer_kernel, experts, images), out_shap...]
where the time goes in v7:
time: 126 us
  Pallas kernels  125 us (99%)
    pallas_call x1, Pallas kernels, body(): pl.pallas_call(functools.partial(layer_kernel, experts, images), out_shap...  119 us
    pallas_call x1, Pallas kernels, finish(): pl.pallas_call(finish_kernel, out_shape=[jax.ShapeDtypeStruct(value.shape...  6.02 us

profile of v7, /device:TPU:1, one launch (start us, length us, event | category | flops | bytes accessed | tf_op | source)
XLA Modules:
  0.0 125.9 jit_solution(2584810882266968938)
XLA Ops:
  0.6 119.0 %layer.1 = (bf16[196,4,768]{2,1,0:T(4,128)(2,1)}, bf16[196,4,768]{2,1,0:T(4,128)(2,1)}, f32[2,768,384]{2,1,0:T(8,128)}, f32[2,384,768]{2,1,0:T(8,128)}, f32[2,768]{1,0:T(2,128)}) custom-call(bf16[196,4,768]{2,1,0:T(4,128)(2,1)} %bitcast.6, bf16[196,4,768]{2,1,0:T(4,128)(2,1)} %bitcast.7, bf16[2,768]{1,0:T(2,128)(2,1)} %bitcast.8, ...), custom_call_target="tpu_custom_call" | custom-call | tf_op jit(solution)/shard_map/layer/pallas_call | solution.py:686
  119.7 6.0 %finish.1 = (bf16[196,4,768]{2,1,0:T(4,128)(2,1)}, bf16[196,4,768]{2,1,0:T(4,128)(2,1)}, f32[2,768,384]{2,1,0:T(8,128)}, f32[2,384,768]{2,1,0:T(8,128)}, f32[2,768]{1,0:T(2,128)}) custom-call(bf16[196,4,768]{2,1,0:T(4,128)(2,1)} %get-tuple-element.15.refs_0_, bf16[196,4,768]{2,1,0:T(4,128)(2,1)} %get-tuple-element.16.refs_1_, ...), custom_call_target="tpu_custom_call" | custom-call | tf_op jit(solution)/shard_map/finish/pallas_call | solution.py:651

commit v8 on v7

--- a/solution.py
+++ b/solution.py
@@ -495,10 +495,12 @@
         w_out_grad[e] = outer(flat(act[e, 0]), flat(rows[1, e]))
         w_in_grad[e] = outer(flat(rows[0, e]), flat(pre_grad[e, 0]))
 
-    def weights_taken(e):
+    def weights_out_taken(e):
         await_bytes(took_out.at[e], swap_recv.at[e, 2])
         w_out_grad[e] = w_out_grad[e] + took_out[e].astype(SINGLE)
         store(w_out_grad.at[e], w_out_grad_hbm.at[e], 4 + e)
+
+    def weights_in_taken(e):
         for k in range(3):
             await_bytes(took_in.at[e, thirds[k]], swap_recv.at[e, 4 + k])
         w_in_grad[e] = w_in_grad[e] + took_in[e].astype(SINGLE)
@@ -558,6 +560,7 @@
         weights_in_given(1, k)
     weights_own(0)
     weights_own(1)
+    weights_out_taken(0)
 
     slot_out = given(0)
     value = outer(combine_low[...], slot_out)[:n_tokens].astype(LOW)
@@ -601,6 +604,8 @@
 
     lax.fori_loop(1, shards, share, 0, unroll=True)
     router_second[dp] = router_mine[...]
+    weights_out_taken(1)
+    weights_in_taken(1)
     await_bytes(router_second.at[pl.ds(0, shards - 1)], a2a_recv.at[6])
     value = jnp.sum(router_second[...], axis=0)
     for s in range(owned):
@@ -608,8 +613,7 @@
             at = s * chunks + c
             router_grad[s : s + 1, c * LANES : (c + 1) * LANES] = value[at : at + 1]
 
-    for e in (1, 0):
-        weights_taken(e)
+    weights_in_taken(0)
     for k in range(4):
         await_bytes(got.at[0, pl.ds(0, experts - 1)], a2a_send.at[k])
     for k in range(4, 6):

time: 126 us -> 125 us (level)
    pallas_call x1, Pallas kernels: 119 us -> 118 us  [body(): pl.pallas_call(functools.partial(layer_kernel, experts, images), out_shap...]
where the time goes in v8:
time: 125 us; the launch traced here: 124 us
  Pallas kernels  124 us (99%)
    pallas_call x1, Pallas kernels, body(): pl.pallas_call(functools.partial(layer_kernel, experts, images), out_shap...  118 us
    pallas_call x1, Pallas kernels, finish(): pl.pallas_call(finish_kernel, out_shape=[jax.ShapeDtypeStruct(value.shape...  6.02 us

profile of v8, /device:TPU:1, one launch (start us, length us, event | category | flops | bytes accessed | tf_op | source)
XLA Modules:
  0.0 124.4 jit_solution(17225321053441667262)
XLA Ops:
  0.6 117.6 %layer.1 = (bf16[196,4,768]{2,1,0:T(4,128)(2,1)}, bf16[196,4,768]{2,1,0:T(4,128)(2,1)}, f32[2,768,384]{2,1,0:T(8,128)}, f32[2,384,768]{2,1,0:T(8,128)}, f32[2,768]{1,0:T(2,128)}) custom-call(bf16[196,4,768]{2,1,0:T(4,128)(2,1)} %bitcast.6, bf16[196,4,768]{2,1,0:T(4,128)(2,1)} %bitcast.7, bf16[2,768]{1,0:T(2,128)(2,1)} %bitcast.8, ...), custom_call_target="tpu_custom_call" | custom-call | tf_op jit(solution)/shard_map/layer/pallas_call | solution.py:690
  118.2 6.0 %finish.1 = (bf16[196,4,768]{2,1,0:T(4,128)(2,1)}, bf16[196,4,768]{2,1,0:T(4,128)(2,1)}, f32[2,768,384]{2,1,0:T(8,128)}, f32[2,384,768]{2,1,0:T(8,128)}, f32[2,768]{1,0:T(2,128)}) custom-call(bf16[196,4,768]{2,1,0:T(4,128)(2,1)} %get-tuple-element.15.refs_0_, bf16[196,4,768]{2,1,0:T(4,128)(2,1)} %get-tuple-element.16.refs_1_, ...), custom_call_target="tpu_custom_call" | custom-call | tf_op jit(solution)/shard_map/finish/pallas_call | solution.py:655
